TPU v7x, 32 devices: a whole 2x2x4 slice. The times are simulated.
32 devices in a mesh: seq: 4 (over z), mp: 8 (over y, x, core).
Axes of the slice: x: 2, y: 2, z: 4, core: 2. Of those that a mesh axis runs over, the one named last changes fastest.
Arguments:
- tokens: bfloat16 [2, 4096, 1536], P(None, ('seq', 'mp')), may hold values from -6 to 6
- cotangent: bfloat16 [2, 4096, 1536], P(None, 'seq'), may hold values from -6 to 6
- w_x: bfloat16 [1536, 2048], P('seq', 'mp'), may hold values from -0.15625 to 0.15625
- w_y: bfloat16 [1536, 2048], P('seq', 'mp'), may hold values from -0.15625 to 0.15625
- w_out: bfloat16 [2048, 1536], P('mp', 'seq'), may hold values from -0.5 to 0.5
- w_gate: bfloat16 [1536, 4608], P('seq', 'mp'), may hold values from -0.15625 to 0.15625
- w_up: bfloat16 [1536, 4608], P('seq', 'mp'), may hold values from -0.15625 to 0.15625
- w_down: bfloat16 [4608, 1536], P('mp', 'seq'), may hold values from -0.1875 to 0.1875
- gate_a: bfloat16 [16, 128, 128], P('mp', 'seq'), may hold values from -0.5 to 0.5
- gate_i: bfloat16 [16, 128, 128], P('mp', 'seq'), may hold values from -0.5 to 0.5
- conv_w: bfloat16 [4, 2048], P(None, ('mp', 'seq')), may hold values from -2 to 2
- decay_param: bfloat16 [2048], P(('mp', 'seq'))
- bias_a: bfloat16 [2048], P(('mp', 'seq')), may hold values from -2 to 2
- bias_i: bfloat16 [2048], P(('mp', 'seq')), may hold values from -2 to 2
- gain_one: bfloat16 [1536], P('seq'), may hold values from 0.099609375 to 1.8984375
- gain_two: bfloat16 [1536], P('seq'), may hold values from 0.099609375 to 1.8984375
- doc_starts: int32 [2, 4], replicated, may hold values from 0 to 4095, as said below
Outputs:
- block_out: bfloat16 [2, 4096, 1536], P(None, ('seq', 'mp'))
- grad_tokens: bfloat16 [2, 4096, 1536], P(None, ('seq', 'mp'))
- grad_w_x: float32 [1536, 2048], P('seq', 'mp')
- grad_w_y: float32 [1536, 2048], P('seq', 'mp')
- grad_w_out: float32 [2048, 1536], P('mp', 'seq')
- grad_w_gate: float32 [1536, 4608], P('seq', 'mp')
- grad_w_up: float32 [1536, 4608], P('seq', 'mp')
- grad_w_down: float32 [4608, 1536], P('mp', 'seq')
- grad_gate_a: float32 [16, 128, 128], P('mp', 'seq')
- grad_gate_i: float32 [16, 128, 128], P('mp', 'seq')
- grad_conv_w: float32 [4, 2048], P(None, ('mp', 'seq'))
- grad_decay_param: float32 [2048], P(('mp', 'seq'))
- grad_bias_a: float32 [2048], P(('mp', 'seq'))
- grad_bias_i: float32 [2048], P(('mp', 'seq'))
- grad_gain_one: float32 [1536], P('seq')
- grad_gain_two: float32 [1536], P('seq')
Inputs may be any that keep to these rules, and one draw needn't show every extreme that they name: `doc_starts`: an entry is a stream position at which a document starts; an entry 0 marks nothing and entries may repeat. In one micro-batch, drawn from the seed, every entry is 0.
All inputs are finite; a program needn't handle non-finite values.
Results may differ from a plain program's by a relative error of at most 0.025.
Values may be sent and summed in bfloat16 or wider, within the bound.
No kernel may reach another device: no remote copies, remote signals or barrier semaphores. Data moves between devices by JAX's collectives and lax.ppermute only.
A program may use at most 128 MiB of HBM per device.

v0:
```python
import jax
import jax.numpy as jnp
from jax import lax
from jax.sharding import PartitionSpec as P

epsilon = 1e-06


def passed_along(block, axis, distance):
    devices = range(lax.axis_size(axis))
    route = [(i - distance, i) for i in devices if i - distance in devices]
    return lax.ppermute(block, axis, route)


def prefix(value, axis, join, neutral, backward):
    count, mine = (lax.axis_size(axis), lax.axis_index(axis))
    pieces = jax.tree.map(lambda part: lax.all_gather(part, axis), value)
    if backward:
        pieces = jax.tree.map(lambda part: part[::-1], pieces)
        mine = count - 1 - mine
    subtotal = jax.tree.map(
        lambda part, zero: jnp.full_like(part, 0) + jnp.asarray(zero, part.dtype), value, neutral
    )

    def turn(position, subtotal):
        longer = join(subtotal, jax.tree.map(lambda part: part[position], pieces))
        return jax.tree.map(lambda new, old: jnp.where(position < mine, new, old), longer, subtotal)

    return lax.fori_loop(0, count - 1, turn, subtotal)


def dense(left_mat, right_mat):
    return jnp.dot(left_mat, right_mat, preferred_element_type=jnp.float32)


def gelu_tanh(values):
    return jax.nn.gelu(values, approximate=True)


def geglu(gate_pre, up_pre):
    return gelu_tanh(gate_pre) * up_pre


def rms_scale(values, gain_vec):
    return (
        values * lax.rsqrt(jnp.mean(values * values, axis=-1, keepdims=True) + epsilon) * gain_vec
    )


def combine_pairs(former, latter):
    return (former[0] * latter[0], latter[0] * former[1] + latter[1])


def conv_mix(padded, conv_taps, tap_masks):
    length = tap_masks.shape[1]
    tap_count = conv_taps.shape[0]
    running = jnp.zeros((length, padded.shape[1]), jnp.float32)
    for offset in range(tap_count):
        window = lax.slice_in_dim(
            padded, tap_count - 1 - offset, tap_count - 1 - offset + length, axis=0
        )
        running = running + conv_taps[offset] * window * tap_masks[offset]
    return running


def gate_terms(conv_out, rate_mat, rate_shift, input_mat, input_shift, decay_in, resets):
    length = conv_out.shape[0]
    groups = rate_mat.shape[0]
    group_width = rate_mat.shape[2]
    blocks = conv_out.reshape(length, groups, group_width)
    rate_pre = (
        jnp.einsum("tnc,ncd->tnd", blocks, rate_mat, precision=lax.Precision.HIGHEST).reshape(
            length, groups * group_width
        )
        + rate_shift
    )
    input_pre = (
        jnp.einsum("tnc,ncd->tnd", blocks, input_mat, precision=lax.Precision.HIGHEST).reshape(
            length, groups * group_width
        )
        + input_shift
    )
    rate_gate = jax.nn.sigmoid(rate_pre)
    input_gate = jax.nn.sigmoid(input_pre)
    log_decay = -8.0 * jax.nn.softplus(decay_in) * rate_gate
    keeps = jnp.exp(log_decay) * (1.0 - resets)
    inflow = jnp.sqrt(-jnp.expm1(2.0 * log_decay)) * input_gate * conv_out
    return (keeps, inflow)


def doc_masks(starts_row, first_pos, length, tap_count):
    active = starts_row > 0
    positions = first_pos + jnp.arange(length, dtype=jnp.int32)

    def counted(places):
        return jnp.sum(
            (active[None, :] & (starts_row[None, :] <= places[:, None])).astype(jnp.int32), axis=1
        )

    current = counted(positions)
    tap_masks = jnp.stack(
        [
            (counted(positions - offset) == current).astype(jnp.float32)[:, None]
            for offset in range(tap_count)
        ]
    )
    resets = jnp.any(starts_row[None, :] == positions[:, None], axis=1).astype(jnp.float32)[:, None]
    return (tap_masks, resets)


def reduce_grads(running):
    gain_sums = lax.psum((running[12], running[13]), "mp")
    return (
        lax.psum_scatter(
            running[0].astype(jnp.bfloat16), "seq", scatter_dimension=0, tiled=True
        ).astype(jnp.float32),
        lax.psum_scatter(
            running[1].astype(jnp.bfloat16), "seq", scatter_dimension=0, tiled=True
        ).astype(jnp.float32),
        lax.psum_scatter(
            running[2].astype(jnp.bfloat16), "seq", scatter_dimension=1, tiled=True
        ).astype(jnp.float32),
        lax.psum_scatter(
            running[3].astype(jnp.bfloat16), "seq", scatter_dimension=0, tiled=True
        ).astype(jnp.float32),
        lax.psum_scatter(
            running[4].astype(jnp.bfloat16), "seq", scatter_dimension=0, tiled=True
        ).astype(jnp.float32),
        lax.psum_scatter(
            running[5].astype(jnp.bfloat16), "seq", scatter_dimension=1, tiled=True
        ).astype(jnp.float32),
        lax.psum_scatter(
            running[6].astype(jnp.bfloat16), "seq", scatter_dimension=1, tiled=True
        ).astype(jnp.float32),
        lax.psum_scatter(
            running[7].astype(jnp.bfloat16), "seq", scatter_dimension=1, tiled=True
        ).astype(jnp.float32),
        lax.psum_scatter(
            running[8].astype(jnp.bfloat16), "seq", scatter_dimension=1, tiled=True
        ).astype(jnp.float32),
        lax.psum_scatter(
            running[9].astype(jnp.bfloat16), "seq", scatter_dimension=0, tiled=True
        ).astype(jnp.float32),
        lax.psum_scatter(
            running[10].astype(jnp.bfloat16), "seq", scatter_dimension=0, tiled=True
        ).astype(jnp.float32),
        lax.psum_scatter(
            running[11].astype(jnp.bfloat16), "seq", scatter_dimension=0, tiled=True
        ).astype(jnp.float32),
        lax.psum_scatter(
            gain_sums[0].astype(jnp.bfloat16), "seq", scatter_dimension=0, tiled=True
        ).astype(jnp.float32),
        lax.psum_scatter(
            gain_sums[1].astype(jnp.bfloat16), "seq", scatter_dimension=0, tiled=True
        ).astype(jnp.float32),
    )


def on_device(
    tokens,
    cotangent,
    w_x,
    w_y,
    w_out,
    w_gate,
    w_up,
    w_down,
    gate_a,
    gate_i,
    conv_w,
    decay_param,
    bias_a,
    bias_i,
    gain_one,
    gain_two,
    doc_starts,
):
    micro_count = tokens.shape[0]
    own_rows = tokens.shape[1]
    span = cotangent.shape[1]
    seq_rank = lax.axis_index("seq")
    mp_rank = lax.axis_index("mp")
    shards = (
        w_x,
        w_y,
        w_out,
        w_gate,
        w_up,
        w_down,
        gate_a,
        gate_i,
        conv_w,
        decay_param,
        bias_a,
        bias_i,
        gain_one,
        gain_two,
    )
    initial = tuple((jnp.zeros(shard.shape, jnp.float32) for shard in shards))
    block_init = jnp.zeros(tokens.shape, jnp.bfloat16)
    grad_init = jnp.zeros(tokens.shape, jnp.bfloat16)

    def micro_step(micro_idx, carry):
        running, block_all, grad_all = carry
        stream = lax.dynamic_index_in_dim(tokens, micro_idx, 0, keepdims=False).astype(jnp.float32)
        cot_block = lax.dynamic_index_in_dim(cotangent, micro_idx, 0, keepdims=False)
        starts_row = lax.dynamic_index_in_dim(doc_starts, micro_idx, 0, keepdims=False)
        gathered = (
            lax.all_gather(w_x, "seq", axis=0, tiled=True),
            lax.all_gather(w_y, "seq", axis=0, tiled=True),
            lax.all_gather(w_out, "seq", axis=1, tiled=True),
            lax.all_gather(w_gate, "seq", axis=0, tiled=True),
            lax.all_gather(w_up, "seq", axis=0, tiled=True),
            lax.all_gather(w_down, "seq", axis=1, tiled=True),
            lax.all_gather(gate_a, "seq", axis=1, tiled=True),
            lax.all_gather(gate_i, "seq", axis=1, tiled=True),
            lax.all_gather(conv_w, "seq", axis=1, tiled=True),
            lax.all_gather(decay_param, "seq", axis=0, tiled=True),
            lax.all_gather(bias_a, "seq", axis=0, tiled=True),
            lax.all_gather(bias_i, "seq", axis=0, tiled=True),
            lax.all_gather(gain_one, "seq", axis=0, tiled=True),
            lax.all_gather(gain_two, "seq", axis=0, tiled=True),
        )
        full_x, full_y, full_out, full_gate, full_up, full_down = gathered[:6]
        small_parts = tuple((piece.astype(jnp.float32) for piece in gathered[6:]))
        mat_a, mat_i, taps_w, decay_w, shift_a, shift_i, scale_one, scale_two = small_parts
        tap_count = taps_w.shape[0]
        tap_masks, resets = doc_masks(starts_row, seq_rank * span, span, tap_count)
        normed_one, pull_one = jax.vjp(rms_scale, stream, scale_one)
        gathered_one = lax.all_gather(normed_one.astype(jnp.bfloat16), "mp", axis=0, tiled=True)
        lru_in = dense(gathered_one, full_x)
        branch_pre = dense(gathered_one, full_y)
        channels = lru_in.shape[1]
        edges = passed_along(lru_in[span - tap_count + 1 :], "seq", 1)
        padded = jnp.concatenate([edges, lru_in], axis=0)
        conv_out, conv_pull = jax.vjp(
            lambda padded_in, taps_in: conv_mix(padded_in, taps_in, tap_masks), padded, taps_w
        )
        (keeps, inflow), gate_pull = jax.vjp(
            lambda conv_in, rate_mat, rate_shift, input_mat, input_shift, decay_in: gate_terms(
                conv_in, rate_mat, rate_shift, input_mat, input_shift, decay_in, resets
            ),
            conv_out,
            mat_a,
            shift_a,
            mat_i,
            shift_i,
            decay_w,
        )
        cumulative, local_state = lax.associative_scan(combine_pairs, (keeps, inflow))
        identity = (jnp.ones((channels,), jnp.float32), jnp.zeros((channels,), jnp.float32))
        arrived = prefix((cumulative[-1], local_state[-1]), "seq", combine_pairs, identity, False)
        entry_state = arrived[1]
        states = local_state + cumulative * entry_state
        branch_act, branch_pull = jax.vjp(gelu_tanh, branch_pre)
        mixed_out = (states * branch_act).astype(jnp.bfloat16)
        middle = stream + lax.psum_scatter(
            dense(mixed_out, full_out).astype(jnp.bfloat16), "mp", scatter_dimension=0, tiled=True
        ).astype(jnp.float32)
        normed_two, pull_two = jax.vjp(rms_scale, middle, scale_two)
        gathered_two = lax.all_gather(normed_two.astype(jnp.bfloat16), "mp", axis=0, tiled=True)
        gate_pre = dense(gathered_two, full_gate)
        up_pre = dense(gathered_two, full_up)
        hidden_full, hidden_pull = jax.vjp(geglu, gate_pre, up_pre)
        hidden = hidden_full.astype(jnp.bfloat16)
        block_rows = (
            middle
            + lax.psum_scatter(
                dense(hidden, full_down).astype(jnp.bfloat16), "mp", scatter_dimension=0, tiled=True
            ).astype(jnp.float32)
        ).astype(jnp.bfloat16)
        cot_rows = lax.dynamic_slice_in_dim(cot_block, mp_rank * own_rows, own_rows, 0).astype(
            jnp.float32
        )
        grad_hidden = dense(cot_block, full_down.T)
        grad_down = dense(hidden.T, cot_block)
        grad_gate_pre, grad_up_pre = hidden_pull(grad_hidden)
        low_gate = grad_gate_pre.astype(jnp.bfloat16)
        low_up = grad_up_pre.astype(jnp.bfloat16)
        grad_gate = dense(gathered_two.T, low_gate)
        grad_up = dense(gathered_two.T, low_up)
        back_two = lax.psum_scatter(
            (dense(low_gate, full_gate.T) + dense(low_up, full_up.T)).astype(jnp.bfloat16),
            "mp",
            scatter_dimension=0,
            tiled=True,
        ).astype(jnp.float32)
        grad_mid_norm, grad_scale_two = pull_two(back_two)
        grad_middle = cot_rows + grad_mid_norm
        gathered_mid = lax.all_gather(grad_middle.astype(jnp.bfloat16), "mp", axis=0, tiled=True)
        grad_out = dense(mixed_out.T, gathered_mid)
        grad_mixed = dense(gathered_mid, full_out.T)
        grad_states = grad_mixed * branch_act
        grad_branch = branch_pull(grad_mixed * states)[0]
        keep_next = jnp.concatenate([keeps[1:], jnp.ones((1, channels), jnp.float32)], axis=0)
        after_prod, local_adj = lax.associative_scan(
            combine_pairs, (keep_next, grad_states), reverse=True
        )
        incoming = prefix(
            (cumulative[-1], keeps[0] * local_adj[0]), "seq", combine_pairs, identity, True
        )
        adjoint = local_adj + after_prod * incoming[1]
        prev_states = jnp.concatenate([entry_state[None, :], states[:-1]], axis=0)
        grad_conv_out, grad_mat_a, grad_shift_a, grad_mat_i, grad_shift_i, grad_decay = gate_pull(
            (adjoint * prev_states, adjoint)
        )
        grad_padded, grad_taps = conv_pull(grad_conv_out)
        back_edges = passed_along(grad_padded[: tap_count - 1], "seq", -1)
        grad_lru = grad_padded[tap_count - 1 :] + jnp.concatenate(
            [jnp.zeros((span - tap_count + 1, channels), jnp.float32), back_edges], axis=0
        )
        low_lru = grad_lru.astype(jnp.bfloat16)
        low_branch = grad_branch.astype(jnp.bfloat16)
        grad_x = dense(gathered_one.T, low_lru)
        grad_y = dense(gathered_one.T, low_branch)
        back_one = lax.psum_scatter(
            (dense(low_lru, full_x.T) + dense(low_branch, full_y.T)).astype(jnp.bfloat16),
            "mp",
            scatter_dimension=0,
            tiled=True,
        ).astype(jnp.float32)
        grad_in_norm, grad_scale_one = pull_one(back_one)
        grad_rows = (grad_middle + grad_in_norm).astype(jnp.bfloat16)
        local_grads = (
            grad_x,
            grad_y,
            grad_out,
            grad_gate,
            grad_up,
            grad_down,
            grad_mat_a,
            grad_mat_i,
            grad_taps,
            grad_decay,
            grad_shift_a,
            grad_shift_i,
            grad_scale_one,
            grad_scale_two,
        )
        local_grads = reduce_grads(local_grads)
        running = tuple(
            (earlier_sum + addition for earlier_sum, addition in zip(running, local_grads))
        )
        block_all = lax.dynamic_update_index_in_dim(block_all, block_rows, micro_idx, 0)
        grad_all = lax.dynamic_update_index_in_dim(grad_all, grad_rows, micro_idx, 0)
        return (running, block_all, grad_all)

    running, block_all, grad_all = lax.fori_loop(
        0, micro_count, micro_step, (initial, block_init, grad_init)
    )
    return (
        block_all,
        grad_all,
        running[0],
        running[1],
        running[2],
        running[3],
        running[4],
        running[5],
        running[6],
        running[7],
        running[8],
        running[9],
        running[10],
        running[11],
        running[12],
        running[13],
    )


def solution(mesh):
    return jax.shard_map(
        on_device,
        mesh=mesh,
        in_specs=(
            P(None, ("seq", "mp"), None),
            P(None, "seq", None),
            P("seq", "mp"),
            P("seq", "mp"),
            P("mp", "seq"),
            P("seq", "mp"),
            P("seq", "mp"),
            P("mp", "seq"),
            P("mp", "seq", None),
            P("mp", "seq", None),
            P(None, ("mp", "seq")),
            P(("mp", "seq")),
            P(("mp", "seq")),
            P(("mp", "seq")),
            P("seq"),
            P("seq"),
            P(),
        ),
        out_specs=(
            P(None, ("seq", "mp"), None),
            P(None, ("seq", "mp"), None),
            P("seq", "mp"),
            P("seq", "mp"),
            P("mp", "seq"),
            P("seq", "mp"),
            P("seq", "mp"),
            P("mp", "seq"),
            P("mp", "seq", None),
            P("mp", "seq", None),
            P(None, ("mp", "seq")),
            P(("mp", "seq")),
            P(("mp", "seq")),
            P(("mp", "seq")),
            P("seq"),
            P("seq"),
        ),
        check_vma=False,
    )
```

profile of v0, /device:TPU:0, one launch (start us, length us, event | category | flops | bytes accessed | tf_op | source)
XLA Modules:
  0.0 2428.6 jit_solution(916704603070876782)
XLA Ops:
  7.3 2414.5 %while.127 = (s32[]{:T(128)}, f32[384,256]{1,0:T(8,128)}, f32[384,256]{1,0:T(8,128)}, f32[256,384]{1,0:T(8,128)}, f32[384,576]{0,1:T(8,128)}, /*index=5*/f32[384...) while((s32[]{:T(128)}, f32[384,256]{1,0:T(8,128)}, ...), condition=%wide.region_43.44_spmd.clone, body=%wide.region_0.43_spmd.clone.sunk | while | flops 26064146432 | bytes 666122560 | solution.py:348
  10.1 13.5 all-gather.18
  25.7 9.9 all-gather.19
  48.7 13.5 all_gather.248
  64.0 19.2 all_gather.251
  83.2 18.7 all_gather.250
  101.9 15.8 all_gather.247
  123.4 13.4 all_gather.249
  271.3 9.3 all-gather.21
  305.4 11.9 all-gather.22
  317.3 31.9 %reduce-scatter.34.cloned.1.call-done = bf16[128,1536]{1,0:T(8,128)(2,1)} async-done(((bf16[1024,1536]{1,0:T(8,128)(2,1)}), bf16[128,1536]{1,0:T(8,128)(2,1)}) %reduce-scatter.34.cloned.1.call-update) | async-done | bytes 393232 | tf_op jit(solution)/shard_map/while/body/eval_jaxpr/reduce_scatter | solution.py:257
  354.2 37.2 %all-gather.37.cloned.1.call-done = bf16[576,1536]{1,0:T(8,128)(2,1)} async-done(((bf16[576,384]{1,0:T(8,128)(2,1)}), bf16[576,1536]{1,0:T(8,128)(2,1)}) %all-gather.37.cloned.1.call-update) | async-done | bytes 1769488 | tf_op jit(solution)/shard_map/while/body/eval_jaxpr/all_gather | solution.py:214
  397.3 35.0 %all-gather.35.cloned.1.call-done = bf16[1536,576]{0,1:T(8,128)(2,1)} async-done(((bf16[384,576]{0,1:T(8,128)(2,1)}), bf16[1536,576]{0,1:T(8,128)(2,1)}) %all-gather.35.cloned.1.call-update) | async-done | bytes 1769488 | tf_op jit(solution)/shard_map/while/body/eval_jaxpr/all_gather | solution.py:212
  432.4 33.0 %all-gather.33.cloned.1.call-done = bf16[1024,1536]{1,0:T(8,128)(2,1)} async-done(((bf16[128,1536]{1,0:T(8,128)(2,1)}), bf16[1024,1536]{1,0:T(8,128)(2,1)}) %all-gather.33.cloned.1.call-update) | async-done | bytes 3145744 | tf_op jit(solution)/shard_map/while/body/eval_jaxpr/all_gather | solution.py:261
  471.3 36.2 %all-gather.39.cloned.1.call-done = bf16[1536,576]{0,1:T(8,128)(2,1)} async-done(((bf16[384,576]{0,1:T(8,128)(2,1)}), bf16[1536,576]{0,1:T(8,128)(2,1)}) %all-gather.39.cloned.1.call-update) | async-done | bytes 1769488 | tf_op jit(solution)/shard_map/while/body/eval_jaxpr/all_gather | solution.py:213
  523.3 45.2 %reduce-scatter.36.cloned.1.call-done = bf16[128,1536]{1,0:T(8,128)(2,1)} async-done(((bf16[1024,1536]{1,0:T(8,128)(2,1)}), bf16[128,1536]{1,0:T(8,128)(2,1)}) %reduce-scatter.36.cloned.1.call-update) | async-done | bytes 393232 | tf_op jit(solution)/shard_map/while/body/eval_jaxpr/reduce_scatter | solution.py:282
  917.2 11.4 all-gather.23
  1029.9 9.7 reduce-scatter.50.cloned.1.call-done
  1040.3 23.0 reduce-scatter.42.cloned.1.call-done
  1064.5 23.5 reduce-scatter.40.cloned.1.call-done
  1089.7 23.0 reduce-scatter.38.cloned.1.call-done
  1114.5 47.4 %reduce-scatter.56.cloned.1.call-done = bf16[128,1536]{1,0:T(8,128)(2,1)} async-done(((bf16[1024,1536]{1,0:T(8,128)(2,1)}), bf16[128,1536]{1,0:T(8,128)(2,1)}) %reduce-scatter.56.cloned.1.call-update) | async-done | bytes 393232 | tf_op jit(solution)/shard_map/while/body/eval_jaxpr/reduce_scatter | solution.py:316
  1163.3 23.1 all-reduce.109
  1186.4 12.0 all-reduce.110
  1198.9 12.7 reduce-scatter.58.cloned.1.call-done
  1218.0 11.9 all-gather.18
  1232.0 9.9 all-gather.19
  1254.9 13.5 all_gather.248
  1270.2 19.1 all_gather.251
  1289.2 18.9 all_gather.250
  1308.2 15.8 all_gather.247
  1329.6 13.4 all_gather.249
  1477.5 9.2 all-gather.21
  1511.5 11.9 all-gather.22
  1523.4 30.7 %reduce-scatter.34.cloned.1.call-done = bf16[128,1536]{1,0:T(8,128)(2,1)} async-done(((bf16[1024,1536]{1,0:T(8,128)(2,1)}), bf16[128,1536]{1,0:T(8,128)(2,1)}) %reduce-scatter.34.cloned.1.call-update) | async-done | bytes 393232 | tf_op jit(solution)/shard_map/while/body/eval_jaxpr/reduce_scatter | solution.py:257
  1559.3 37.0 %all-gather.37.cloned.1.call-done = bf16[576,1536]{1,0:T(8,128)(2,1)} async-done(((bf16[576,384]{1,0:T(8,128)(2,1)}), bf16[576,1536]{1,0:T(8,128)(2,1)}) %all-gather.37.cloned.1.call-update) | async-done | bytes 1769488 | tf_op jit(solution)/shard_map/while/body/eval_jaxpr/all_gather | solution.py:214
  1602.3 35.2 %all-gather.35.cloned.1.call-done = bf16[1536,576]{0,1:T(8,128)(2,1)} async-done(((bf16[384,576]{0,1:T(8,128)(2,1)}), bf16[1536,576]{0,1:T(8,128)(2,1)}) %all-gather.35.cloned.1.call-update) | async-done | bytes 1769488 | tf_op jit(solution)/shard_map/while/body/eval_jaxpr/all_gather | solution.py:212
  1637.5 33.0 %all-gather.33.cloned.1.call-done = bf16[1024,1536]{1,0:T(8,128)(2,1)} async-done(((bf16[128,1536]{1,0:T(8,128)(2,1)}), bf16[1024,1536]{1,0:T(8,128)(2,1)}) %all-gather.33.cloned.1.call-update) | async-done | bytes 3145744 | tf_op jit(solution)/shard_map/while/body/eval_jaxpr/all_gather | solution.py:261
  1676.4 36.4 %all-gather.39.cloned.1.call-done = bf16[1536,576]{0,1:T(8,128)(2,1)} async-done(((bf16[384,576]{0,1:T(8,128)(2,1)}), bf16[1536,576]{0,1:T(8,128)(2,1)}) %all-gather.39.cloned.1.call-update) | async-done | bytes 1769488 | tf_op jit(solution)/shard_map/while/body/eval_jaxpr/all_gather | solution.py:213
  1728.5 45.1 %reduce-scatter.36.cloned.1.call-done = bf16[128,1536]{1,0:T(8,128)(2,1)} async-done(((bf16[1024,1536]{1,0:T(8,128)(2,1)}), bf16[128,1536]{1,0:T(8,128)(2,1)}) %reduce-scatter.36.cloned.1.call-update) | async-done | bytes 393232 | tf_op jit(solution)/shard_map/while/body/eval_jaxpr/reduce_scatter | solution.py:282
  2122.4 11.3 all-gather.23
  2245.5 23.1 reduce-scatter.42.cloned.1.call-done
  2269.9 23.6 reduce-scatter.40.cloned.1.call-done
  2295.3 22.9 reduce-scatter.38.cloned.1.call-done
  2320.1 47.3 %reduce-scatter.56.cloned.1.call-done = bf16[128,1536]{1,0:T(8,128)(2,1)} async-done(((bf16[1024,1536]{1,0:T(8,128)(2,1)}), bf16[128,1536]{1,0:T(8,128)(2,1)}) %reduce-scatter.56.cloned.1.call-update) | async-done | bytes 393232 | tf_op jit(solution)/shard_map/while/body/eval_jaxpr/reduce_scatter | solution.py:316
  2368.8 23.1 all-reduce.109
  2391.9 12.0 all-reduce.110
  2404.4 12.7 reduce-scatter.58.cloned.1.call-done
  (1533 shorter events, 1367.7 us)
Async XLA Ops:
  7.6 110.1 %all-gather.31.cloned.1.call-start = ((), (), s32[]{:S(2)}) async-start(), calls=%async_computation.13 | async-start | bytes 3538944 | tf_op jit(solution)/shard_map/while/body/eval_jaxpr/all_gather | solution.py:230
  25.7 323.6 %reduce-scatter.34.cloned.1.call-start = ((), (), s32[]{:S(2)}) async-start(), calls=%async_computation.14 | async-start | bytes 3538944 | tf_op jit(solution)/shard_map/while/body/eval_jaxpr/reduce_scatter | solution.py:257
  120.9 15.9 collective-permute-start
  304.0 87.5 %all-gather.37.cloned.1.call-start = ((), (), s32[]{:S(2)}) async-start(), calls=%async_computation.17 | async-start | bytes 2211840 | tf_op jit(solution)/shard_map/while/body/eval_jaxpr/all_gather | solution.py:214
  304.7 127.7 %all-gather.35.cloned.1.call-start = ((), (), s32[]{:S(2)}) async-start(), calls=%async_computation.16 | async-start | bytes 2211840 | tf_op jit(solution)/shard_map/while/body/eval_jaxpr/all_gather | solution.py:212
  305.3 160.1 %all-gather.33.cloned.1.call-start = ((), (), s32[]{:S(2)}) async-start(), calls=%async_computation.15 | async-start | bytes 3538944 | tf_op jit(solution)/shard_map/while/body/eval_jaxpr/all_gather | solution.py:261
  353.6 153.9 %all-gather.39.cloned.1.call-start = ((), (), s32[]{:S(2)}) async-start(), calls=%async_computation.18 | async-start | bytes 2211840 | tf_op jit(solution)/shard_map/while/body/eval_jaxpr/all_gather | solution.py:213
  354.2 214.3 %reduce-scatter.36.cloned.1.call-start = ((), (), s32[]{:S(2)}) async-start(), calls=%async_computation.19 | async-start | bytes 3538944 | tf_op jit(solution)/shard_map/while/body/eval_jaxpr/reduce_scatter | solution.py:282
  523.2 108.5 %all-gather.41.cloned.1.call-start = ((), (), s32[]{:S(2)}) async-start(), calls=%async_computation.20 | async-start | bytes 3538944 | tf_op jit(solution)/shard_map/while/body/eval_jaxpr/all_gather | solution.py:290
  574.0 447.6 %reduce-scatter.48.cloned.1.call-start = ((), (), s32[]{:S(2)}) async-start(), calls=%async_computation.26 | async-start | bytes 2457600 | tf_op jit(solution)/shard_map/while
  583.5 439.5 %reduce-scatter.46.cloned.1.call-start = ((), (), s32[]{:S(2)}) async-start(), calls=%async_computation.25 | async-start | bytes 2457600 | tf_op jit(solution)/shard_map/while
  593.1 431.2 %reduce-scatter.44.cloned.1.call-start = ((), (), s32[]{:S(2)}) async-start(), calls=%async_computation.24 | async-start | bytes 2457600 | tf_op jit(solution)/shard_map/while
  631.6 396.7 %reduce-scatter.54.cloned.1.call-start = ((), (), s32[]{:S(2)}) async-start(), calls=%async_computation.29 | async-start | bytes 81920 | tf_op jit(solution)/shard_map/while
  984.4 44.8 %reduce-scatter.52.cloned.1.call-start = ((), (), s32[]{:S(2)}) async-start(), calls=%async_computation.28 | async-start | bytes 81920 | tf_op jit(solution)/shard_map/while/body/eval_jaxpr/reduce_scatter | solution.py:135
  987.4 52.1 %reduce-scatter.50.cloned.1.call-start = ((), (), s32[]{:S(2)}) async-start(), calls=%async_computation.27 | async-start | bytes 81920 | tf_op jit(solution)/shard_map/while/body/eval_jaxpr/reduce_scatter | solution.py:132
  989.3 74.0 %reduce-scatter.42.cloned.1.call-start = ((), (), s32[]{:S(2)}) async-start(), calls=%async_computation.23 | async-start | bytes 983040 | tf_op jit(solution)/shard_map/while
  995.7 92.3 %reduce-scatter.40.cloned.1.call-start = ((), (), s32[]{:S(2)}) async-start(), calls=%async_computation.22 | async-start | bytes 983040 | tf_op jit(solution)/shard_map/while/body/eval_jaxpr/reduce_scatter | solution.py:117
  998.8 114.0 %reduce-scatter.38.cloned.1.call-start = ((), (), s32[]{:S(2)}) async-start(), calls=%async_computation.21 | async-start | bytes 983040 | tf_op jit(solution)/shard_map/while/body/eval_jaxpr/reduce_scatter | solution.py:114
  1000.5 5.9 collective-permute-start.1
  1009.0 152.9 %reduce-scatter.56.cloned.1.call-start = ((), (), s32[]{:S(2)}) async-start(), calls=%async_computation.30 | async-start | bytes 3538944 | tf_op jit(solution)/shard_map/while/body/eval_jaxpr/reduce_scatter | solution.py:316
  1014.3 197.3 %reduce-scatter.58.cloned.1.call-start = ((), (), s32[]{:S(2)}) async-start(), calls=%async_computation.31 | async-start | bytes 3538944 | tf_op jit(solution)/shard_map/while/body/eval_jaxpr/reduce_scatter | solution.py:268
  1028.2 183.4 %copy-start.23 = (bf16[128,1536]{1,0:T(8,128)(2,1)S(1)}, bf16[128,1536]{1,0:T(8,128)(2,1)}, u32[]{:S(2)}) copy-start(bf16[128,1536]{1,0:T(8,128)(2,1)} %reduce-scatter.36.cloned.1.call-done) | copy-start | bytes 1179652 | tf_op jit(solution)/shard_map/while
  1028.2 183.4 %copy-start.81 = (f32[128]{0:T(128)S(1)}, f32[128]{0:T(128)}, u32[]{:S(2)}) copy-start(f32[128]{0:T(128)} %copy-done.80) | copy-start | bytes 1540 | tf_op jit(solution)/shard_map/while
  1028.2 183.4 %copy-start.104 = (f32[128]{0:T(128)S(1)}, f32[128]{0:T(128)}, u32[]{:S(2)}) copy-start(f32[128]{0:T(128)} %copy-done.103) | copy-start | bytes 1540 | tf_op jit(solution)/shard_map/while
  1029.1 185.2 %copy-start.102 = (f32[4,64]{1,0:T(4,128)}, f32[4,64]{1,0:T(4,128)S(1)}, u32[]{:S(2)}) copy-start(f32[4,64]{1,0:T(4,128)S(1)} %select_add_fusion.30) | copy-start | bytes 3076 | tf_op jit(solution)/shard_map/while
  1029.9 184.5 %copy-start.65 = (f32[2,32,128]{2,1,0:T(8,128)}, f32[2,32,128]{2,1,0:T(8,128)S(1)}, u32[]{:S(2)}) copy-start(f32[2,32,128]{2,1,0:T(8,128)S(1)} %select_add_fusion.29) | copy-start | bytes 98308 | tf_op jit(solution)/shard_map/while
  1215.5 108.5 %all-gather.31.cloned.1.call-start = ((), (), s32[]{:S(2)}) async-start(), calls=%async_computation.13 | async-start | bytes 3538944 | tf_op jit(solution)/shard_map/while/body/eval_jaxpr/all_gather | solution.py:230
  1231.9 322.3 %reduce-scatter.34.cloned.1.call-start = ((), (), s32[]{:S(2)}) async-start(), calls=%async_computation.14 | async-start | bytes 3538944 | tf_op jit(solution)/shard_map/while/body/eval_jaxpr/reduce_scatter | solution.py:257
  1327.2 15.8 collective-permute-start
  1510.0 86.4 %all-gather.37.cloned.1.call-start = ((), (), s32[]{:S(2)}) async-start(), calls=%async_computation.17 | async-start | bytes 2211840 | tf_op jit(solution)/shard_map/while/body/eval_jaxpr/all_gather | solution.py:214
  1510.7 126.7 %all-gather.35.cloned.1.call-start = ((), (), s32[]{:S(2)}) async-start(), calls=%async_computation.16 | async-start | bytes 2211840 | tf_op jit(solution)/shard_map/while/body/eval_jaxpr/all_gather | solution.py:212
  1511.5 159.1 %all-gather.33.cloned.1.call-start = ((), (), s32[]{:S(2)}) async-start(), calls=%async_computation.15 | async-start | bytes 3538944 | tf_op jit(solution)/shard_map/while/body/eval_jaxpr/all_gather | solution.py:261
  1558.5 154.2 %all-gather.39.cloned.1.call-start = ((), (), s32[]{:S(2)}) async-start(), calls=%async_computation.18 | async-start | bytes 2211840 | tf_op jit(solution)/shard_map/while/body/eval_jaxpr/all_gather | solution.py:213
  1559.3 214.3 %reduce-scatter.36.cloned.1.call-start = ((), (), s32[]{:S(2)}) async-start(), calls=%async_computation.19 | async-start | bytes 3538944 | tf_op jit(solution)/shard_map/while/body/eval_jaxpr/reduce_scatter | solution.py:282
  1728.4 108.4 %all-gather.41.cloned.1.call-start = ((), (), s32[]{:S(2)}) async-start(), calls=%async_computation.20 | async-start | bytes 3538944 | tf_op jit(solution)/shard_map/while/body/eval_jaxpr/all_gather | solution.py:290
  1779.2 447.6 %reduce-scatter.48.cloned.1.call-start = ((), (), s32[]{:S(2)}) async-start(), calls=%async_computation.26 | async-start | bytes 2457600 | tf_op jit(solution)/shard_map/while
  1788.7 439.4 %reduce-scatter.46.cloned.1.call-start = ((), (), s32[]{:S(2)}) async-start(), calls=%async_computation.25 | async-start | bytes 2457600 | tf_op jit(solution)/shard_map/while
  1798.3 431.1 %reduce-scatter.44.cloned.1.call-start = ((), (), s32[]{:S(2)}) async-start(), calls=%async_computation.24 | async-start | bytes 2457600 | tf_op jit(solution)/shard_map/while
  1836.8 398.1 %reduce-scatter.54.cloned.1.call-start = ((), (), s32[]{:S(2)}) async-start(), calls=%async_computation.29 | async-start | bytes 81920 | tf_op jit(solution)/shard_map/while
  2189.6 46.3 %reduce-scatter.52.cloned.1.call-start = ((), (), s32[]{:S(2)}) async-start(), calls=%async_computation.28 | async-start | bytes 81920 | tf_op jit(solution)/shard_map/while/body/eval_jaxpr/reduce_scatter | solution.py:135
  2192.6 52.2 %reduce-scatter.50.cloned.1.call-start = ((), (), s32[]{:S(2)}) async-start(), calls=%async_computation.27 | async-start | bytes 81920 | tf_op jit(solution)/shard_map/while/body/eval_jaxpr/reduce_scatter | solution.py:132
  2194.4 74.2 %reduce-scatter.42.cloned.1.call-start = ((), (), s32[]{:S(2)}) async-start(), calls=%async_computation.23 | async-start | bytes 983040 | tf_op jit(solution)/shard_map/while
  2200.9 92.6 %reduce-scatter.40.cloned.1.call-start = ((), (), s32[]{:S(2)}) async-start(), calls=%async_computation.22 | async-start | bytes 983040 | tf_op jit(solution)/shard_map/while/body/eval_jaxpr/reduce_scatter | solution.py:117
  2203.9 114.4 %reduce-scatter.38.cloned.1.call-start = ((), (), s32[]{:S(2)}) async-start(), calls=%async_computation.21 | async-start | bytes 983040 | tf_op jit(solution)/shard_map/while/body/eval_jaxpr/reduce_scatter | solution.py:114
  2205.7 5.9 collective-permute-start.1
  2214.2 153.3 %reduce-scatter.56.cloned.1.call-start = ((), (), s32[]{:S(2)}) async-start(), calls=%async_computation.30 | async-start | bytes 3538944 | tf_op jit(solution)/shard_map/while/body/eval_jaxpr/reduce_scatter | solution.py:316
  2219.5 197.6 %reduce-scatter.58.cloned.1.call-start = ((), (), s32[]{:S(2)}) async-start(), calls=%async_computation.31 | async-start | bytes 3538944 | tf_op jit(solution)/shard_map/while/body/eval_jaxpr/reduce_scatter | solution.py:268
  2235.8 184.1 %copy-start.102 = (f32[4,64]{1,0:T(4,128)}, f32[4,64]{1,0:T(4,128)S(1)}, u32[]{:S(2)}) copy-start(f32[4,64]{1,0:T(4,128)S(1)} %select_add_fusion.30) | copy-start | bytes 3076 | tf_op jit(solution)/shard_map/while
  (244 other events, 8318.6 us)
Sparse Core Ops, SparseCore 0:
  25.8 32.0 all-gather.30
  304.1 45.0 reduce-scatter.33
  350.9 40.5 all-gather.36
  393.0 39.3 all-gather.34
  434.3 31.1 all-gather.32
  467.0 40.5 all-gather.38
  523.3 45.0 reduce-scatter.35
  574.1 32.2 all-gather.40
  608.8 41.4 reduce-scatter.47
  652.5 40.6 reduce-scatter.45
  695.5 40.6 reduce-scatter.43
  984.5 16.2 reduce-scatter.53
  1003.2 17.1 reduce-scatter.51
  1022.4 17.1 reduce-scatter.49
  1041.7 21.5 reduce-scatter.41
  1065.4 22.5 reduce-scatter.39
  1090.2 22.5 reduce-scatter.37
  1116.4 45.5 reduce-scatter.55
  1165.3 46.2 reduce-scatter.57
  1232.0 31.0 all-gather.30
  1510.1 44.0 reduce-scatter.33
  1555.8 40.5 all-gather.36
  1598.1 39.3 all-gather.34
  1639.4 31.1 all-gather.32
  1672.2 40.5 all-gather.38
  1728.6 45.0 reduce-scatter.35
  1779.3 32.3 all-gather.40
  1814.0 41.4 reduce-scatter.47
  1857.8 40.6 reduce-scatter.45
  1900.7 40.6 reduce-scatter.43
  2189.7 16.2 reduce-scatter.53
  2208.3 17.1 reduce-scatter.51
  2227.6 17.1 reduce-scatter.49
  2247.1 21.4 reduce-scatter.41
  2270.9 22.5 reduce-scatter.39
  2295.7 22.5 reduce-scatter.37
  2321.9 45.5 reduce-scatter.55
  2370.8 46.2 reduce-scatter.57
where the time goes:
time: 2460 us; the launch traced here: 2430 us
  local copies, waits for them, and re-layouts  784 us (32%)
  waiting for transfers between devices  726 us (30%)
  blocking collectives  375 us (15%)
  other arithmetic  327 us (13%)
  matrix products  182 us (7%)
    slice x146, local copies, waits for them, and re-layouts, micro_step(): lax.associative_scan(combine_pairs, (keep_next, grad_states), reverse=True)  271 us
    pad x72, local copies, waits for them, and re-layouts, micro_step(): lax.associative_scan(combine_pairs, (keep_next, grad_states), reverse=True)  171 us
    dot_general x36, matrix products, dense(): return jnp.dot(left_mat, right_mat, preferred_element_type=jnp.float32)  158 us
    slice x136, local copies, waits for them, and re-layouts, micro_step(): lax.associative_scan(combine_pairs, (keeps, inflow))  106 us
    reduce_scatter x2, waiting for transfers between devices, micro_step(): lax.psum_scatter((dense(low_lru, full_x.T) + dense(low_branch, full_y.T))...  94.8 us
    reduce_scatter x2, waiting for transfers between devices, micro_step(): lax.psum_scatter((dense(low_gate, full_gate.T) + dense(low_up, full_up.T)...  90.3 us
    while x544, local copies, waits for them, and re-layouts  82.4 us
    pad x72, local copies, waits for them, and re-layouts, micro_step(): lax.associative_scan(combine_pairs, (keeps, inflow))  76.1 us
  transfers between devices with their start and end apart: 42, of which 26 were waited for; matrix products, arithmetic and copies ran while one was open for 38% of the time, Pallas kernels for 0%

commit v1 on v0

v1 whole, which is shorter than its diff:
```python
import functools

import jax
import jax.numpy as jnp
from jax import lax
from jax.experimental import pallas as pl
from jax.experimental.pallas import tpu as pltpu
from jax.sharding import PartitionSpec as P

epsilon = 1e-06
SEGS = 8
WIDE = 128
TILE = 128
ROOT = 0.7978845608028654
CUBE = 0.044715


def gelu_pair(v):
    inner = ROOT * v * (1.0 + CUBE * v * v)
    t = jnp.tanh(inner)
    half = 0.5 * (1.0 + t)
    slope = half + 0.5 * v * (1.0 - t * t) * (ROOT * (1.0 + (3.0 * CUBE) * v * v))
    return v * half, slope


def gelu_only(v):
    return v * (0.5 + 0.5 * jnp.tanh(ROOT * v * (1.0 + CUBE * v * v)))


def swapped(x, flips):
    rows = lax.broadcasted_iota(jnp.int32, x.shape, 0)
    for bit in (1, 2, 4):
        down, up = pltpu.roll(x, SEGS - bit, 0), pltpu.roll(x, bit, 0)
        turned = jnp.where((rows & bit) == 0, down, up)
        x = jnp.where((flips & bit) != 0, turned, x)
    return x


def exclusive(prod, last, flips, backward):
    prod, last = swapped(prod, flips), swapped(last, flips)
    one = jnp.ones((1, WIDE), jnp.float32)
    zero = jnp.zeros((1, WIDE), jnp.float32)
    coef, base = [one], [zero]
    order = range(SEGS - 1, -1, -1) if backward else range(SEGS)
    for s in order:
        coef.append(prod[s : s + 1] * coef[-1])
        base.append(prod[s : s + 1] * base[-1] + last[s : s + 1])
    total = jnp.concatenate([coef[-1], base[-1]] + [zero] * (SEGS - 2), axis=0)
    coef, base = coef[:-1], base[:-1]
    if backward:
        coef, base = coef[::-1], base[::-1]
    return (
        swapped(jnp.concatenate(coef, axis=0), flips),
        swapped(jnp.concatenate(base, axis=0), flips),
        total,
    )


def enter_kernel(
    where, u, edge, code, small, gates, inter, v_out, rg_out, ig_out, e_out, sq_out, maps, total
):
    rows = u.shape[0]
    steps = rows // SEGS
    flips = where[0]

    def lay(s, carry):
        inter[pl.ds(pl.multiple_of(24 + 8 * s, 8), 8), :] = u[pl.ds(s, 8, stride=steps), :]
        return carry

    lax.fori_loop(0, steps, lay, 0, unroll=8)
    first = lax.broadcasted_iota(jnp.int32, (SEGS, WIDE), 0) == 0
    for j in range(3):
        nat = pltpu.roll(swapped(inter[pl.ds(8 * (steps + j), 8), :], flips), 1, 0)
        nat = jnp.where(first, edge[5 + j : 6 + j, :], nat)
        inter[8 * j : 8 * j + 8, :] = swapped(nat, flips)

    def tile(i, carry):
        prod, state = carry
        base = pl.multiple_of(i * TILE, TILE)
        c = code[pl.ds(base, TILE), :]
        v = small[0:1, :] * inter[pl.ds(base + 24, TILE), :]
        for k in (1, 2, 3):
            v = v + jnp.where(
                c >= k, small[k : k + 1, :] * inter[pl.ds(base + 24 - 8 * k, TILE), :], 0.0
            )
        high = v.astype(jnp.bfloat16)
        low = (v - high.astype(jnp.float32)).astype(jnp.bfloat16)
        mat = gates[0]
        pre = jnp.dot(
            jnp.concatenate([high, low], axis=1),
            jnp.concatenate([mat, mat], axis=0),
            preferred_element_type=jnp.float32,
        )
        rg = 1.0 / (1.0 + jnp.exp(-(pre[:, :WIDE] + small[5:6, :])))
        ig = jax.nn.sigmoid(pre[:, WIDE:] + small[6:7, :])
        la = small[4:5, :] * rg
        e = jnp.exp(la)
        sq = jnp.sqrt(jnp.tanh(-la) * (1.0 + e * e))
        here = pl.ds(base, TILE)
        v_out[here, :] = v
        rg_out[here, :] = rg
        ig_out[here, :] = ig
        e_out[here, :] = e
        sq_out[here, :] = sq
        keep = jnp.where(c > 0, e, 0.0)
        inflow = sq * ig * v
        for s in range(TILE // SEGS):
            k = keep[8 * s : 8 * s + 8]
            prod = prod * k
            state = k * state + inflow[8 * s : 8 * s + 8]
        return prod, state

    prod, state = lax.fori_loop(
        0,
        rows // TILE,
        tile,
        (jnp.ones((SEGS, WIDE), jnp.float32), jnp.zeros((SEGS, WIDE), jnp.float32)),
    )
    coef, base, whole = exclusive(prod, state, flips, False)
    maps[0:8, :] = prod
    maps[8:16, :] = coef
    maps[16:24, :] = base
    total[...] = whole


def state_kernel(count, where, v, ig, e, sq, code, p, maps, *rest):
    others, (hs, out, wide) = rest[: count - 1], rest[count - 1 :]
    rows = v.shape[0]
    steps = rows // SEGS
    mine = where[1]
    entry = jnp.zeros((1, WIDE), jnp.float32)
    for d in range(count - 1, 0, -1):
        piece = others[d - 1]
        entry = jnp.where(mine >= d, piece[0:1, :] * entry + piece[1:2, :], entry)
    state = maps[8:16, :] * entry + maps[16:24, :]
    hs[0:8, :] = state

    def tile(i, state):
        base = pl.multiple_of(i * TILE, TILE)
        here = pl.ds(base, TILE)
        keep = jnp.where(code[here, :] > 0, e[here, :], 0.0)
        inflow = sq[here, :] * ig[here, :] * v[here, :]
        for s in range(TILE // SEGS):
            state = keep[8 * s : 8 * s + 8] * state + inflow[8 * s : 8 * s + 8]
            hs[pl.ds(base + 8 * s + 8, 8), :] = state
            there = pl.ds(i * (TILE // SEGS) + s, 8, stride=steps)
            wide[there, :] = state * gelu_only(p[there, :])
        return state

    lax.fori_loop(0, rows // TILE, tile, state)
    out[...] = wide[...].astype(jnp.bfloat16)


def adjoint_kernel(where, do, p, hs, e, code, maps, dhs, dp, back, total, wide):
    rows = do.shape[0]
    steps = rows // SEGS
    flips = where[0]

    def tile(i, grad):
        i = rows // TILE - 1 - i
        base = pl.multiple_of(i * TILE, TILE)
        keep = jnp.where(code[pl.ds(base, TILE), :] > 0, e[pl.ds(base, TILE), :], 0.0)
        for s in range(TILE // SEGS - 1, -1, -1):
            there = pl.ds(i * (TILE // SEGS) + s, 8, stride=steps)
            d = do[there, :]
            act, slope = gelu_pair(p[there, :])
            wide[there, :] = d * hs[pl.ds(base + 8 * s + 8, 8), :] * slope
            dh = d * act
            dhs[pl.ds(base + 8 * s, 8), :] = dh
            grad = keep[8 * s : 8 * s + 8] * (dh + grad)
        return grad

    grad = lax.fori_loop(0, rows // TILE, tile, jnp.zeros((SEGS, WIDE), jnp.float32))
    dp[...] = wide[...].astype(jnp.bfloat16)
    coef, base, whole = exclusive(maps[0:8, :], grad, flips, True)
    back[0:8, :] = coef
    back[8:16, :] = base
    total[...] = whole


def leave_kernel(count, where, dhs, inter, v, rg, ig, e, sq, hs, code, small, gates_t, back, *rest):
    products, grads = rest[: count - 1], rest[count - 1 : 2 * count - 2]
    du, grad_gates, sums, edge, dv_all, wide = rest[2 * count - 2 :]
    rows = dhs.shape[0]
    steps = rows // SEGS
    flips, mine = where[0], where[1]
    entry = jnp.zeros((1, WIDE), jnp.float32)
    for j in range(count - 1, 0, -1):
        d = count - j
        entry = jnp.where(
            mine + j < count, products[d - 1][0:1, :] * entry + grads[d - 1][1:2, :], entry
        )
    grad = back[0:8, :] * entry + back[8:16, :]
    grad_gates[...] = jnp.zeros_like(grad_gates)

    def fold(x):
        parts = [x[8 * s : 8 * s + 8] for s in range(TILE // SEGS)]
        while len(parts) > 1:
            parts = [a + b for a, b in zip(parts[::2], parts[1::2])]
        return parts[0]

    def tile(i, carry):
        grad, taps, decay, shift_a, shift_i = carry
        i = rows // TILE - 1 - i
        base = pl.multiple_of(i * TILE, TILE)
        here = pl.ds(base, TILE)
        c = code[here, :]
        e_now, sq_now, rg_now, ig_now, v_now = e[here, :], sq[here, :], rg[here, :], ig[here, :], v[here, :]
        keep = jnp.where(c > 0, e_now, 0.0)
        d_now = dhs[here, :]
        pieces = [None] * (TILE // SEGS)
        for s in range(TILE // SEGS - 1, -1, -1):
            a = d_now[8 * s : 8 * s + 8] + grad
            pieces[s] = a
            grad = keep[8 * s : 8 * s + 8] * a
        a = jnp.concatenate(pieces, axis=0)
        q = ig_now * v_now
        dla = a * (keep * hs[here, :] - q * (e_now * e_now) / jnp.maximum(sq_now, 1e-25))
        rate = rg_now * dla
        decay = decay + fold(rate)
        dra = small[4:5, :] * rate * (1.0 - rg_now)
        asq = a * sq_now
        dia = asq * q * (1.0 - ig_now)
        shift_a = shift_a + fold(dra)
        shift_i = shift_i + fold(dia)
        both = jnp.concatenate([dra.astype(jnp.bfloat16), dia.astype(jnp.bfloat16)], axis=1)
        dv = asq * ig_now + jnp.dot(both, gates_t[0], preferred_element_type=jnp.float32)
        grad_gates[0] += lax.dot_general(
            v_now.astype(jnp.bfloat16),
            both,
            (((0,), (0,)), ((), ())),
            preferred_element_type=jnp.float32,
        )
        dv_all[here, :] = dv
        new_taps = [taps[0] + fold(dv * inter[pl.ds(base + 24, TILE), :])]
        for k in (1, 2, 3):
            new_taps.append(
                taps[k]
                + fold(jnp.where(c >= k, dv * inter[pl.ds(base + 24 - 8 * k, TILE), :], 0.0))
            )
        return grad, tuple(new_taps), decay, shift_a, shift_i

    zero = jnp.zeros((SEGS, WIDE), jnp.float32)
    _, taps, decay, shift_a, shift_i = lax.fori_loop(
        0, rows // TILE, tile, (grad, (zero,) * 4, zero, zero, zero)
    )
    totals = [jnp.sum(x, axis=0, keepdims=True) for x in (*taps, decay, shift_a, shift_i)]
    sums[...] = jnp.concatenate(totals + [jnp.zeros((1, WIDE), jnp.float32)], axis=0)
    last = lax.broadcasted_iota(jnp.int32, (SEGS, WIDE), 0) == SEGS - 1
    edges = []
    for j in range(3):
        nat = swapped(dv_all[8 * j : 8 * j + 8, :], flips)
        edges.append(nat[0:1])
        nat = jnp.where(last, 0.0, pltpu.roll(nat, SEGS - 1, 0))
        dv_all[pl.ds(rows + 8 * j, 8), :] = swapped(nat, flips)
    edge[...] = jnp.concatenate(edges + [jnp.zeros((SEGS - 3, WIDE), jnp.float32)], axis=0)

    def mix(i, carry):
        base = pl.multiple_of(i * TILE, TILE)
        total = small[0:1, :] * dv_all[pl.ds(base, TILE), :]
        for k in (1, 2, 3):
            there = pl.ds(base + 8 * k, TILE)
            total = total + jnp.where(
                code[there, :] >= k, small[k : k + 1, :] * dv_all[there, :], 0.0
            )
        for s in range(TILE // SEGS):
            wide[pl.ds(i * (TILE // SEGS) + s, 8, stride=steps), :] = total[8 * s : 8 * s + 8]
        return carry

    lax.fori_loop(0, rows // TILE, mix, 0)
    du[...] = wide[...].astype(jnp.bfloat16)


def lanes(rows, offset=0):
    return pl.BlockSpec((rows, WIDE), lambda n: (0, n + offset))


def per_block(shape):
    return pl.BlockSpec((1,) + shape, lambda n: (n, 0, 0))


def scalars():
    return pl.BlockSpec(memory_space=pltpu.SMEM)


def shared(shape):
    return pl.BlockSpec(shape, lambda n: (0,) * len(shape))


def launch(kernel, groups, in_specs, outs, scratch, args, ops, name):
    moved = sum(a.size * a.dtype.itemsize for a in args) + sum(
        functools.reduce(lambda x, y: x * y, s, 1) * jnp.dtype(t).itemsize for s, t, _ in outs
    )
    return pl.pallas_call(
        kernel,
        grid=(groups,),
        in_specs=in_specs,
        out_specs=[spec for _, _, spec in outs],
        out_shape=[jax.ShapeDtypeStruct(shape, dtype) for shape, dtype, _ in outs],
        scratch_shapes=scratch,
        compiler_params=pltpu.CompilerParams(vmem_limit_bytes=40 * 2**20),
        cost_estimate=pl.CostEstimate(flops=ops, bytes_accessed=moved, transcendentals=ops // 20),
        name=name,
    )(*args)


def enter(where, both, edge, code, small, gates):
    rows, channels = both.shape[0], both.shape[1] // 2
    groups = channels // WIDE
    f32 = jnp.float32
    full = ((rows, channels), f32, lanes(rows))
    return launch(
        enter_kernel,
        groups,
        [scalars(), lanes(rows), lanes(8), shared(code.shape), lanes(8), per_block((WIDE, 2 * WIDE))],
        [
            ((rows + 24, channels), f32, lanes(rows + 24)),
            full,
            full,
            full,
            full,
            full,
            ((24, channels), f32, lanes(24)),
            ((8, channels), f32, lanes(8)),
        ],
        [],
        (where, both, edge, code, small, gates),
        rows * channels * 600,
        "enter",
    )


def states_of(where, v, ig, e, sq, code, both, maps, others):
    rows, channels = v.shape
    groups = channels // WIDE
    f32 = jnp.float32
    return launch(
        functools.partial(state_kernel, len(others) + 1),
        groups,
        [scalars()]
        + [lanes(rows)] * 4
        + [shared(code.shape), lanes(rows, groups), lanes(24)]
        + [lanes(8)] * len(others),
        [
            ((rows + 8, channels), f32, lanes(rows + 8)),
            ((rows, channels), jnp.bfloat16, lanes(rows)),
        ],
        [pltpu.VMEM((rows, WIDE), f32)],
        (where, v, ig, e, sq, code, both, maps, *others),
        rows * channels * 60,
        "states",
    )


def adjoints(where, do, both, hs, e, code, maps):
    rows, channels = do.shape
    groups = channels // WIDE
    f32 = jnp.float32
    return launch(
        adjoint_kernel,
        groups,
        [
            scalars(),
            lanes(rows),
            lanes(rows, groups),
            lanes(rows + 8),
            lanes(rows),
            shared(code.shape),
            lanes(24),
        ],
        [
            ((rows, channels), f32, lanes(rows)),
            ((rows, channels), jnp.bfloat16, lanes(rows)),
            ((16, channels), f32, lanes(16)),
            ((8, channels), f32, lanes(8)),
        ],
        [pltpu.VMEM((rows, WIDE), f32)],
        (where, do, both, hs, e, code, maps),
        rows * channels * 80,
        "adjoint",
    )


def leave(where, dhs, kept, hs, code, small, gates_t, back, products, grads):
    inter, v, rg, ig, e, sq = kept
    rows, channels = dhs.shape
    groups = channels // WIDE
    f32 = jnp.float32
    count = len(products) + 1
    return launch(
        functools.partial(leave_kernel, count),
        groups,
        [scalars(), lanes(rows), lanes(rows + 24)]
        + [lanes(rows)] * 5
        + [
            lanes(rows + 8),
            shared(code.shape),
            lanes(8),
            per_block((2 * WIDE, WIDE)),
            lanes(16),
        ]
        + [lanes(8)] * (2 * count - 2),
        [
            ((rows, channels), jnp.bfloat16, lanes(rows)),
            ((groups, WIDE, 2 * WIDE), f32, per_block((WIDE, 2 * WIDE))),
            ((8, channels), f32, lanes(8)),
            ((8, channels), f32, lanes(8)),
        ],
        [pltpu.VMEM((rows + 24, WIDE), f32), pltpu.VMEM((rows, WIDE), f32)],
        (where, dhs, inter, v, rg, ig, e, sq, hs, code, small, gates_t, back, *products, *grads),
        rows * channels * 900,
        "leave",
    )


def dense(left_mat, right_mat):
    return jnp.dot(left_mat, right_mat, preferred_element_type=jnp.float32)


def dense_nt(left_mat, right_mat):
    return lax.dot_general(
        left_mat, right_mat, (((1,), (1,)), ((), ())), preferred_element_type=jnp.float32
    )


def dense_tn(left_mat, right_mat):
    return lax.dot_general(
        left_mat, right_mat, (((0,), (0,)), ((), ())), preferred_element_type=jnp.float32
    )


def low(x):
    return x.astype(jnp.bfloat16)


def turned(x, axis, distance):
    count = lax.axis_size(axis)
    return lax.ppermute(x, axis, [(i, (i + distance) % count) for i in range(count)])


def around(x, axis):
    return [turned(x, axis, d) for d in range(1, lax.axis_size(axis))]


def flip(x, bits):
    count = lax.axis_size("mp")
    return lax.ppermute(x, "mp", [(i, i ^ bits) for i in range(count)])


class Paired:
    halves = 2

    def spread(self, rows):
        return jnp.concatenate([rows] + [flip(rows, bits) for bits in (2, 4, 6)], axis=0)

    def collect(self, count, part):
        size = count // 4
        blocks = [slice(size * b, size * (b + 1)) for b in range(4)]
        far = [flip(low(part(blocks[b])), 2 * b) for b in (3, 1, 2)]
        total = part(blocks[0])
        for piece in far:
            total = total + piece.astype(jnp.float32)
        return total

    def both(self, x, axis):
        return jnp.concatenate([x, flip(x, 1)], axis=axis)

    def own_sum(self, x, axis):
        size = x.shape[axis] // 2
        mine = lax.slice_in_dim(x, 0, size, axis=axis)
        other = low(lax.slice_in_dim(x, size, 2 * size, axis=axis))
        return mine + flip(other, 1).astype(jnp.float32)


class Plain:
    halves = 1

    def spread(self, rows):
        return lax.all_gather(rows, "mp", axis=0, tiled=True)

    def collect(self, count, part):
        return lax.psum_scatter(
            low(part(slice(0, count))), "mp", scatter_dimension=0, tiled=True
        ).astype(jnp.float32)

    def both(self, x, axis):
        return x

    def own_sum(self, x, axis):
        return x


def mask_code(starts_row, first_pos, flips, steps):
    segs = lax.broadcasted_iota(jnp.int32, (steps + 3, SEGS), 1)
    step = lax.broadcasted_iota(jnp.int32, (steps + 3, SEGS), 0)
    places = first_pos + (segs ^ flips) * steps + step
    code = jnp.full(places.shape, 4, jnp.int32)
    for e in range(starts_row.shape[0]):
        start = starts_row[e]
        code = jnp.where(
            (start > 0) & (places >= start), jnp.minimum(code, places - start), code
        )
    code = code.astype(jnp.float32).reshape(-1, 1)
    return jnp.broadcast_to(code, (code.shape[0], WIDE))


def normed(rows):
    scale = lax.rsqrt(jnp.mean(rows * rows, axis=-1, keepdims=True) + epsilon)
    return rows * scale, scale


def norm_back(grad_norm, norm, scale):
    return scale * (grad_norm - norm * jnp.mean(grad_norm * norm, axis=-1, keepdims=True))


def micro(plan, where, flips, stream, cot, cot_rows, starts_row, weights):
    wx, wy, wo, wg, wu, wd, gates, taps, decay, shift_a, shift_i, gain_one, gain_two = weights
    count = cot.shape[0]
    steps = count // SEGS
    seq_rank = lax.axis_index("seq")
    channels = wo.shape[0]
    hidden = wd.shape[0]
    code = mask_code(starts_row, seq_rank * count, flips, steps)
    rate = -8.0 * jax.nn.softplus(decay)
    small = jnp.concatenate(
        [taps, rate[None], shift_a[None], shift_i[None], jnp.zeros((1, channels), jnp.float32)],
        axis=0,
    )
    gates_t = jnp.concatenate(
        [gates[:, :, :WIDE].transpose(0, 2, 1), gates[:, :, WIDE:].transpose(0, 2, 1)], axis=1
    )

    n1, s1 = normed(stream)
    h1 = plan.spread(low(n1 * gain_one))
    last = lax.dynamic_slice_in_dim(h1, ((SEGS - 1) ^ flips) * steps + steps - 8, 8, 0)
    before = turned(last, "seq", 1)
    edge = jnp.where(seq_rank > 0, dense_nt(before, wx), 0.0)
    up_both = dense_nt(h1, jnp.concatenate([wx, wy], axis=0))
    *kept, maps, total = enter(where, up_both, edge, code, small, gates)
    inter, v, rg, ig, e, sq = kept
    fore = around(total, "seq")
    hs, mixed = states_of(where, v, ig, e, sq, code, up_both, maps, fore)

    middle = stream + plan.collect(count, lambda rows: dense(mixed[rows], wo))
    n2, s2 = normed(middle)
    h2 = plan.spread(low(n2 * gain_two))
    gate_pre = dense_nt(h2, wg)
    up_pre = dense_nt(h2, wu)
    act, slope = gelu_pair(gate_pre)
    mid = low(act * up_pre)
    grad_mid = dense_nt(cot, wd)
    low_gate = low(grad_mid * up_pre * slope)
    low_up = low(grad_mid * act)

    back_two = plan.collect(
        count, lambda rows: dense(low_gate[rows], wg) + dense(low_up[rows], wu)
    )
    block_rows = low(middle + plan.collect(count, lambda rows: dense(mid[rows], wd)))
    grad_wd = dense_tn(mid, cot)
    grad_wg = dense_tn(low_gate, h2)
    grad_wu = dense_tn(low_up, h2)
    grad_middle = cot_rows + norm_back(back_two * gain_two, n2, s2)
    mid_rows = plan.spread(low(grad_middle))
    do = dense_nt(mid_rows, wo)
    grad_wo = dense_tn(mixed, mid_rows)
    dhs, dp, back, total = adjoints(where, do, up_both, hs, e, code, maps)
    aft = around(total, "seq")
    du, grad_gates, sums, edge = leave(
        where, dhs, kept, hs, code, small, gates_t, back, fore, aft
    )
    nxt = jnp.where(
        seq_rank < lax.axis_size("seq") - 1, turned(edge, "seq", -1), 0.0
    )
    own = ((SEGS - 1) ^ flips) * steps
    after = seq_rank * count + count
    far = jnp.full((3,), 4, jnp.int32)
    for i in range(starts_row.shape[0]):
        places = after + jnp.arange(3, dtype=jnp.int32)
        start = starts_row[i]
        far = jnp.where((start > 0) & (places >= start), jnp.minimum(far, places - start), far)
    extra = []
    for j in range(3):
        row = jnp.zeros((channels,), jnp.float32)
        for k in range(3 - j, 4):
            row = row + jnp.where(far[j + k - 3] >= k, taps[k] * nxt[j + k - 3], 0.0)
        extra.append(row)
    extra = jnp.concatenate([jnp.zeros((5, channels), jnp.float32), jnp.stack(extra)], axis=0)
    at = own + steps - 8
    patch = low(lax.dynamic_slice_in_dim(du, at, 8, 0).astype(jnp.float32) + extra)
    du = lax.dynamic_update_slice_in_dim(du, patch, at, 0)
    back_one = plan.collect(count, lambda rows: dense(du[rows], wx) + dense(dp[rows], wy))
    grad_wx = dense_tn(du, h1)
    grad_wy = dense_tn(dp, h1)
    grad_rows = low(grad_middle + norm_back(back_one * gain_one, n1, s1))
    grad_one = (
        jnp.sum(grad_wx * wx.astype(jnp.float32) + grad_wy * wy.astype(jnp.float32), axis=0)
        / gain_one
    )
    grad_two = (
        jnp.sum(grad_wg * wg.astype(jnp.float32) + grad_wu * wu.astype(jnp.float32), axis=0)
        / gain_two
    )
    large = (grad_wx, grad_wy, grad_wo, grad_wg, grad_wu, grad_wd)
    decay_sum = -8.0 * jax.nn.sigmoid(decay) * sums[4]
    lines = jnp.concatenate([sums[:4], decay_sum[None], sums[5:7]], axis=0)
    return block_rows, grad_rows, large, (grad_gates, lines, jnp.stack([grad_one, grad_two]))


def on_device(
    tokens,
    cotangent,
    w_x,
    w_y,
    w_out,
    w_gate,
    w_up,
    w_down,
    gate_a,
    gate_i,
    conv_w,
    decay_param,
    bias_a,
    bias_i,
    gain_one,
    gain_two,
    doc_starts,
):
    micros, own_rows, _ = tokens.shape
    span = cotangent.shape[1]
    count = lax.axis_size("seq")
    seq_rank = lax.axis_index("seq")
    mp_rank = lax.axis_index("mp")
    paired = micros == 2 and lax.axis_size("mp") == SEGS and span == SEGS * own_rows
    plan = Paired() if paired else Plain()
    channels, hidden = w_x.shape[1], w_gate.shape[1]
    blocks, depth, _ = gate_a.shape
    part = w_x.shape[0]
    thin = conv_w.shape[1]

    flat = jnp.concatenate(
        [a.reshape(-1) for a in (gate_a, gate_i, conv_w, decay_param, bias_a, bias_i, gain_one, gain_two)]
    )
    rows = -(-flat.shape[0] // (16 * part)) * 16
    packed = jnp.pad(flat, (0, rows * part - flat.shape[0])).reshape(rows, part)
    first = lax.all_gather(
        jnp.concatenate([w_x.T, w_y.T, packed], axis=0), "seq", axis=1, tiled=True
    )
    second = lax.all_gather(
        jnp.concatenate([w_out, w_gate.T, w_up.T, w_down], axis=0), "seq", axis=1, tiled=True
    )
    if paired:
        firsts, seconds = [first, flip(first, 1)], [second, flip(second, 1)]
    else:
        firsts, seconds = [first], [second]

    def join(arrays, begin, size):
        return jnp.concatenate([a[begin : begin + size] for a in arrays], axis=0)

    wx, wy = join(firsts, 0, channels), join(firsts, channels, channels)
    wo = join(seconds, 0, channels)
    wg = join(seconds, channels, hidden)
    wu = join(seconds, channels + hidden, hidden)
    wd = join(seconds, channels + 2 * hidden, hidden)
    smalls = []
    for a in firsts:
        a = a[2 * channels :].reshape(rows, count, part).transpose(1, 0, 2).reshape(count, -1)
        at, found = 0, []
        for shape in (gate_a.shape, gate_i.shape, conv_w.shape, (thin,), (thin,), (thin,), (part,), (part,)):
            size = 1
            for n in shape:
                size *= n
            found.append(a[:, at : at + size].reshape((count,) + shape))
            at += size
        ga, gi, cw, dp, ba, bi, g1, g2 = found
        ga, gi = (x.transpose(1, 0, 2, 3).reshape(blocks, count * depth, WIDE) for x in (ga, gi))
        cw = cw.transpose(1, 0, 2).reshape(conv_w.shape[0], channels)
        smalls.append((jnp.concatenate([ga, gi], axis=2), cw, dp.reshape(-1), ba.reshape(-1), bi.reshape(-1)))
    gain_1, gain_2 = (g.reshape(-1).astype(jnp.float32) for g in (g1, g2))
    gates = jnp.concatenate([s[0] for s in smalls], axis=0)
    taps = jnp.concatenate([s[1] for s in smalls], axis=1).astype(jnp.float32)
    decay, shift_a, shift_i = (
        jnp.concatenate([s[i] for s in smalls], axis=0).astype(jnp.float32) for i in (2, 3, 4)
    )
    weights = (wx, wy, wo, wg, wu, wd, gates, taps, decay, shift_a, shift_i, gain_1, gain_2)

    if paired:
        core = mp_rank % 2
        mine = lax.dynamic_index_in_dim(tokens, core, 0, keepdims=False)
        other = flip(lax.dynamic_index_in_dim(tokens, 1 - core, 0, keepdims=False), 1)
        stream = jnp.concatenate([mine, other], axis=0).astype(jnp.float32)
        cot = lax.dynamic_index_in_dim(cotangent, core, 0, keepdims=False)
        cot = cot.reshape(SEGS, own_rows, -1)
        cot = jnp.concatenate(
            [lax.dynamic_index_in_dim(cot, s ^ mp_rank, 0, keepdims=False) for s in range(SEGS)],
            axis=0,
        )
        where = jnp.stack([mp_rank, seq_rank]).astype(jnp.int32)
        starts_row = lax.dynamic_index_in_dim(doc_starts, core, 0, keepdims=False)
        block_rows, grad_rows, large, little = micro(
            plan, where, mp_rank, stream, cot, cot[: 2 * own_rows].astype(jnp.float32), starts_row, weights
        )

        def returned(x):
            mine, other = x[:own_rows], flip(x[own_rows:], 1)
            return jnp.where(core == 0, jnp.stack([mine, other]), jnp.stack([other, mine]))

        block_all, grad_all = returned(block_rows), returned(grad_rows)
    else:
        where = jnp.stack([0 * seq_rank, seq_rank]).astype(jnp.int32)
        found = []
        for m in range(micros):
            stream = tokens[m].astype(jnp.float32)
            cot_rows = lax.dynamic_slice_in_dim(cotangent[m], mp_rank * own_rows, own_rows, 0)
            found.append(
                micro(plan, where, 0, stream, cotangent[m], cot_rows.astype(jnp.float32), doc_starts[m], weights)
            )
        block_all = jnp.stack([f[0] for f in found])
        grad_all = jnp.stack([f[1] for f in found])
        large, little = jax.tree.map(lambda *x: sum(x), *[f[2:] for f in found])

    grad_wx, grad_wy, grad_wo, grad_wg, grad_wu, grad_wd = large

    def owned(*grads):
        own = [low(plan.own_sum(g, 0)) for g in grads]
        return lax.psum_scatter(
            jnp.concatenate(own, axis=0), "seq", scatter_dimension=1, tiled=True
        ).astype(jnp.float32)

    late = owned(grad_wx, grad_wy)
    early = owned(grad_wg, grad_wu, grad_wd)
    out_grad = owned(grad_wo)

    grad_gates, lines, gains = little
    if paired:
        grad_gates = grad_gates[:blocks] + flip(grad_gates[blocks:], 1)
        lines = lines[:, :channels] + flip(lines[:, channels:], 1)
    pieces = jnp.concatenate(
        [
            grad_gates.reshape(blocks, count, depth, 2 * WIDE).transpose(1, 0, 2, 3).reshape(count, -1),
            lines.reshape(-1, count, thin).transpose(1, 0, 2).reshape(count, -1),
            gains.reshape(2, count, part).transpose(1, 0, 2).reshape(count, -1),
        ],
        axis=1,
    )
    size = pieces.shape[1]
    pieces = jnp.pad(pieces, ((0, 0), (0, -size % 1024))).reshape(count, -1, WIDE)
    total = lax.dynamic_index_in_dim(pieces, seq_rank, 0, keepdims=False)
    for d in range(1, count):
        piece = lax.dynamic_index_in_dim(pieces, (seq_rank + d) % count, 0, keepdims=False)
        total = total + turned(piece, "seq", d)
    total = total.reshape(-1)
    at = blocks * depth * 2 * WIDE
    sum_gates = total[:at].reshape(blocks, depth, 2, WIDE)
    lines = total[at : at + 7 * thin].reshape(7, thin)
    at += 7 * thin
    gains = total[at : at + 2 * part].reshape(2, part)
    if paired:
        for bits in (1, 2, 4):
            gains = gains + flip(gains, bits)
    else:
        gains = lax.psum(gains, "mp")
    return (
        block_all,
        grad_all,
        late[:channels].T,
        late[channels:].T,
        out_grad,
        early[:hidden].T,
        early[hidden : 2 * hidden].T,
        early[2 * hidden :],
        sum_gates[:, :, 0],
        sum_gates[:, :, 1],
        lines[:4],
        lines[4],
        lines[5],
        lines[6],
        gains[0],
        gains[1],
    )


def solution(mesh):
    return jax.shard_map(
        on_device,
        mesh=mesh,
        in_specs=(
            P(None, ("seq", "mp"), None),
            P(None, "seq", None),
            P("seq", "mp"),
            P("seq", "mp"),
            P("mp", "seq"),
            P("seq", "mp"),
            P("seq", "mp"),
            P("mp", "seq"),
            P("mp", "seq", None),
            P("mp", "seq", None),
            P(None, ("mp", "seq")),
            P(("mp", "seq")),
            P(("mp", "seq")),
            P(("mp", "seq")),
            P("seq"),
            P("seq"),
            P(),
        ),
        out_specs=(
            P(None, ("seq", "mp"), None),
            P(None, ("seq", "mp"), None),
            P("seq", "mp"),
            P("seq", "mp"),
            P("mp", "seq"),
            P("seq", "mp"),
            P("seq", "mp"),
            P("mp", "seq"),
            P("mp", "seq", None),
            P("mp", "seq", None),
            P(None, ("mp", "seq")),
            P(("mp", "seq")),
            P(("mp", "seq")),
            P(("mp", "seq")),
            P("seq"),
            P("seq"),
        ),
        check_vma=False,
    )
```

time: 2460 us -> 678 us (0.28)
  local copies, waits for them, and re-layouts: 784 us -> 88.7 us
  waiting for transfers between devices: 726 us -> 325 us
  blocking collectives: 375 us -> 0 us
  other arithmetic: 327 us -> 37.2 us
  matrix products: 182 us -> 113 us
  Pallas kernels: 0 us -> 38 us
  starting transfers between devices: 10.1 us -> 46.5 us
    reduce_scatter x16 -> x0, waiting for transfers between devices: 384 us -> none  [the longest x2 94.8 us: micro_step(): lax.psum_scatter((dense(low_lru, full_x.T) + dense(low_branch, full_y.T))...]
    slice x288 -> x32, local copies, waits for them, and re-layouts: 380 us -> 27.9 us  [the longest x6 12.9 us: join(): return jnp.concatenate([a[begin:begin + size] for a in arrays], axis=0)]
    all_gather x22 -> x0, blocking collectives: 288 us -> none  [the longest x6 58 us: prefix(): pieces = jax.tree.map(lambda part: lax.all_gather(part, axis), value)]
    pad x144 -> x1, local copies, waits for them, and re-layouts: 247 us -> 0.01 us  [on_device(): packed = jnp.pad(flat, (0, rows * part - flat.shape[0])).reshape(rows, part)]
    ppermute x4 -> x48, waiting for transfers between devices: 7.75 us -> 187 us  [the longest x37 177 us: flip(): return lax.ppermute(x, 'mp', [(i, i ^ bits) for i in range(count)])]
    all_gather x12 -> x2, waiting for transfers between devices: 283 us -> 132 us  [the longest x1 113 us: on_device(): lax.all_gather(jnp.concatenate([w_out, w_gate.T, w_up.T, w_down], axis=0)...]
    add x144 -> x7, other arithmetic: 126 us -> 0.08 us  [the longest x1 0.04 us: on_device(): grad_gates = grad_gates[:blocks] + flip(grad_gates[blocks:], 1)]
    dot_general x36 -> x24, matrix products: 158 us -> 45.8 us  [dense(): return jnp.dot(left_mat, right_mat, preferred_element_type=jnp.float32)]
  transfers between devices with their start and end apart: 42 -> 53, of which waited for: 26 -> 23; matrix products, arithmetic and copies ran while one was open for 38% -> 26% of each run, Pallas kernels for 0% -> 6%
where the time goes in v1:
time: 678 us; the launch traced here: 670 us
  waiting for transfers between devices  325 us (48%)
  matrix products  113 us (17%)
  local copies, waits for them, and re-layouts  88.7 us (13%)
  starting transfers between devices  46.5 us (7%)
  Pallas kernels  38 us (6%)
  other arithmetic  37.2 us (5%)
  between operations  22.3 us (3%)
    ppermute x37, waiting for transfers between devices, flip(): return lax.ppermute(x, 'mp', [(i, i ^ bits) for i in range(count)])  177 us
    all_gather x1, waiting for transfers between devices, on_device(): lax.all_gather(jnp.concatenate([w_out, w_gate.T, w_up.T, w_down], axis=0)...  113 us
    dot_general x24, matrix products, dense(): return jnp.dot(left_mat, right_mat, preferred_element_type=jnp.float32)  45.8 us
    unnamed x220, local copies, waits for them, and re-layouts  43.1 us
    dot_general x6, matrix products, dense_nt(): lax.dot_general(left_mat, right_mat, (((1,), (1,)), ((), ())), preferred_...  38.1 us
    pallas_call x4, Pallas kernels, launch(): pl.pallas_call(kernel, grid=(groups,), in_specs=in_specs, out_specs=[spec...  38 us
    ppermute x37, starting transfers between devices, flip(): return lax.ppermute(x, 'mp', [(i, i ^ bits) for i in range(count)])  30.9 us
    dot_general x6, matrix products, dense_tn(): lax.dot_general(left_mat, right_mat, (((0,), (0,)), ((), ())), preferred_...  28.7 us
  transfers between devices with their start and end apart: 53, of which 23 were waited for; matrix products, arithmetic and copies ran while one was open for 26% of the time, Pallas kernels for 6%

profile of v1, /device:TPU:0, one launch (start us, length us, event | category | flops | bytes accessed | tf_op | source)
XLA Modules:
  0.0 670.2 jit_solution(3378833875137561476)
XLA Ops:
  8.0 4.9 concatenate.130
  16.1 2.6 pad_maximum_fusion.11
  25.2 2.5 fusion.93
  39.2 19.4 %all-gather.3.cloned.1.call-done = bf16[560,1536]{1,0:T(8,128)(2,1)} async-done(((bf16[560,384]{1,0:T(8,128)(2,1)}), bf16[560,1536]{1,0:T(8,128)(2,1)}) %all-gather.3.cloned.1.call-update) | async-done | bytes 1720336 | tf_op jit(solution)/shard_map/all_gather | solution.py:645
  58.6 112.6 %all-gather.5.cloned.1.call-done = bf16[1984,1536]{1,0:T(8,128)(2,1)} async-done(((bf16[1984,384]{1,0:T(8,128)(2,1)}), bf16[1984,1536]{1,0:T(8,128)(2,1)}) %all-gather.5.cloned.1.call-update) | async-done | bytes 6094864 | tf_op jit(solution)/shard_map/all_gather | solution.py:648
  180.4 2.4 collective-permute-start.4
  186.7 15.0 %collective-permute-done.4 = bf16[256,1536]{1,0:T(8,128)(2,1)S(1)} collective-permute-done((bf16[256,1536]{1,0:T(8,128)(2,1)S(1)}, bf16[256,1536]{1,0:T(8,128)(2,1)S(1)}, u32[]{:S(2)}, u32[]{:S(2)}) %collective-permute-start.4) | collective-permute-done | bytes 786464 | tf_op jit(solution)/shard_map/ppermute | solution.py:447
  201.7 16.4 %collective-permute-done.3 = bf16[256,1536]{1,0:T(8,128)(2,1)S(1)} collective-permute-done((bf16[256,1536]{1,0:T(8,128)(2,1)S(1)}, bf16[256,1536]{1,0:T(8,128)(2,1)S(1)}, u32[]{:S(2)}, u32[]{:S(2)}) %collective-permute-start.3) | collective-permute-done | bytes 786464 | tf_op jit(solution)/shard_map/ppermute | solution.py:447
  219.6 6.7 %fusion.13.u.p = f32[1024,1024]{1,0:T(8,128)} fusion(bf16[1024,1536]{1,0:T(8,128)(2,1)S(1)} %pad_maximum_fusion.4, bf16[256,1536]{1,0:T(8,128)(2,1)S(1)} %get-tuple-element.120, bf16[256,1536]{1,0:T(8,128)(2,1)S(1)} %copy-done.59, bf16[256,1536]{1,0:T(8,128)(2,1)S(1)} %get-tuple-element.119, bf16[256,1536]{1,0:T(8,128)(2,1)S(1)} %copy-done.55), kind=kOutput, calls=%fused_computation.30 | convolution fusion | flops 3233808384 | bytes 10485760 | tf_op jit(solution)/shard_map/dot_general | solution.py:421
  227.1 12.8 %enter.1 = (f32[1048,512]{1,0:T(8,128)S(1)}, f32[1024,512]{1,0:T(8,128)S(1)}, f32[1024,512]{1,0:T(8,128)S(1)}, f32[1024,512]{1,0:T(8,128)S(1)}, f32[1024,512]{1,...) custom-call(s32[2]{0:T(128)S(1)} %pad_add_fusion.where, ...), custom_call_target="tpu_custom_call" | custom-call | flops 314572800 | bytes 17723400 | tf_op jit(solution)/shard_map/enter/pallas_call | solution.py:294
  247.7 3.2 collective-permute-start.7
  251.1 2.5 and_select_fusion.3
  259.6 6.0 states.1
  275.8 5.4 fusion.119
  281.2 9.1 %collective-permute-done.12 = bf16[256,1536]{1,0:T(8,128)(2,1)S(1)} collective-permute-done((bf16[256,1536]{1,0:T(8,128)(2,1)S(1)}, bf16[256,1536]{1,0:T(8,128)(2,1)S(1)}, u32[]{:S(2)}, u32[]{:S(2)}) %collective-permute-start.12) | collective-permute-done | bytes 786464 | tf_op jit(solution)/shard_map/ppermute | solution.py:447
  292.5 13.7 %collective-permute-done.10 = bf16[256,1536]{1,0:T(8,128)(2,1)S(1)} collective-permute-done((bf16[256,1536]{1,0:T(8,128)(2,1)S(1)}, bf16[256,1536]{1,0:T(8,128)(2,1)S(1)}, u32[]{:S(2)}, u32[]{:S(2)}) %collective-permute-start.10) | collective-permute-done | bytes 786464 | tf_op jit(solution)/shard_map/ppermute | solution.py:447
  311.9 8.3 %fusion.113 = f32[1024,1152]{1,0:T(8,128)} fusion(bf16[1024,1536]{1,0:T(8,128)(2,1)} %bitcast_dynamic-update-slice_fusion, bf16[576,1536]{1,0:T(8,128)(2,1)S(1)} %get-tuple-element.112, bf16[576,1536]{1,0:T(8,128)(2,1)S(1)} %get-tuple-element.109), kind=kOutput, calls=%fused_computation.248 | convolution fusion | flops 3630956544 | bytes 11403264 | tf_op jit(solution)/shard_map/dot_general | solution.py:421
  320.2 9.6 %collective-permute-done.15 = bf16[256,1536]{1,0:T(8,128)(2,1)S(1)} collective-permute-done((bf16[256,1536]{1,0:T(8,128)(2,1)S(1)}, bf16[256,1536]{1,0:T(8,128)(2,1)S(1)}, u32[]{:S(2)}, u32[]{:S(2)}) %collective-permute-start.15) | collective-permute-done | bytes 786464 | tf_op jit(solution)/shard_map/ppermute | solution.py:447
  329.8 12.6 %collective-permute-done.14 = bf16[256,1536]{1,0:T(8,128)(2,1)S(1)} collective-permute-done((bf16[256,1536]{1,0:T(8,128)(2,1)S(1)}, bf16[256,1536]{1,0:T(8,128)(2,1)S(1)}, u32[]{:S(2)}, u32[]{:S(2)}) %collective-permute-start.14) | collective-permute-done | bytes 786464 | tf_op jit(solution)/shard_map/ppermute | solution.py:447
  342.5 6.4 fusion.114
  348.9 14.3 %fusion.8 = (bf16[1024,1152]{1,0:T(8,128)(2,1)}, bf16[1024,1152]{1,0:T(8,128)(2,1)}, bf16[1024,1152]{1,0:T(8,128)(2,1)}) fusion(f32[1024,1152]{1,0:T(8,128)} %fusion.113, f32[1024,1152]{1,0:T(8,128)} %fusion.114, bf16[576,1536]{1,0:T(8,128)(2,1)} %get-tuple-element.114, bf16[576,1536]{1,0:T(8,128)(2,1)S(1)} %copy-done.45, bf16[256,1536]{1,0:T(8,128)(2,1)} %copy-done.81, ...), kind=kOutput, calls=%fused_computation.12 | convolution fusion | flops 3673030656 | bytes 23199744 | tf_op jit(solution)/shard_map/dot_general | solution.py:421
  382.1 7.7 %collective-permute-done.22 = bf16[256,1536]{1,0:T(8,128)(2,1)S(1)} collective-permute-done((bf16[256,1536]{1,0:T(8,128)(2,1)S(1)}, bf16[256,1536]{1,0:T(8,128)(2,1)S(1)}, u32[]{:S(2)}, u32[]{:S(2)}) %collective-permute-start.22) | collective-permute-done | bytes 786464 | tf_op jit(solution)/shard_map/ppermute | solution.py:447
  389.9 3.6 collective-permute-done.21
  393.5 15.7 %collective-permute-done.20 = bf16[256,1536]{1,0:T(8,128)(2,1)S(1)} collective-permute-done((bf16[256,1536]{1,0:T(8,128)(2,1)S(1)}, bf16[256,1536]{1,0:T(8,128)(2,1)S(1)}, u32[]{:S(2)}, u32[]{:S(2)}) %collective-permute-start.20) | collective-permute-done | bytes 786464 | tf_op jit(solution)/shard_map/ppermute | solution.py:447
  414.8 5.8 fusion.129
  422.1 10.5 %collective-permute-done.25 = bf16[256,1536]{1,0:T(8,128)(2,1)S(1)} collective-permute-done((bf16[256,1536]{1,0:T(8,128)(2,1)S(1)}, bf16[256,1536]{1,0:T(8,128)(2,1)S(1)}, u32[]{:S(2)}, u32[]{:S(2)}) %collective-permute-start.25) | collective-permute-done | bytes 786464 | tf_op jit(solution)/shard_map/ppermute | solution.py:447
  432.7 14.7 %collective-permute-done.24 = bf16[256,1536]{1,0:T(8,128)(2,1)S(1)} collective-permute-done((bf16[256,1536]{1,0:T(8,128)(2,1)S(1)}, bf16[256,1536]{1,0:T(8,128)(2,1)S(1)}, u32[]{:S(2)}, u32[]{:S(2)}) %collective-permute-start.24) | collective-permute-done | bytes 786464 | tf_op jit(solution)/shard_map/ppermute | solution.py:447
  449.2 7.2 %adjoint.1 = (f32[1024,512]{1,0:T(8,128)S(1)}, bf16[1024,512]{1,0:T(8,128)(2,1)S(1)}, f32[16,512]{1,0:T(8,128)S(1)}, f32[8,512]{1,0:T(8,128)S(1)}) custom-call(s32[2]{0:T(128)S(1)} %pad_add_fusion.where, f32[1024,512]{1,0:T(8,128)S(1)} %fusion.72.do, f32[1024,1024]{1,0:T(8,128)S(1)} %copy-done.2, f32[1032,512]{1,0:T(8,128)S(1)} %get-tuple-element.41.hs, ...), custom_call_target="tpu_custom_call" | custom-call | flops 41943040 | bytes 14282760 | tf_op jit(solution)/shard_map/adjoint/pallas_call | solution.py:294
  456.5 2.6 collective-permute-start.26
  461.7 7.6 %fusion.117 = f32[1152,1536]{1,0:T(8,128)} fusion(bf16[1024,1152]{1,0:T(8,128)(2,1)} %get-tuple-element.106, bf16[256,1536]{1,0:T(8,128)(2,1)S(1)} %copy-done.82, bf16[256,1536]{1,0:T(8,128)(2,1)S(1)} %copy-done.84, bf16[256,1536]{1,0:T(8,128)(2,1)S(1)} %copy-done.86, bf16[256,1536]{1,0:T(8,128)(2,1)S(1)} %copy-done.70), kind=kOutput, calls=%fused_computation.252 | convolution fusion | flops 3636461568 | bytes 12582912 | tf_op jit(solution)/shard_map/dot_general | solution.py:427
  469.4 12.0 %leave.1 = (bf16[1024,512]{1,0:T(8,128)(2,1)S(1)}, f32[4,128,256]{2,1,0:T(8,128)S(1)}, f32[8,512]{1,0:T(8,128)S(1)}, f32[8,512]{1,0:T(8,128)S(1)}) custom-call(s32[2]{0:T(128)S(1)} %pad_add_fusion.where, f32[1024,512]{1,0:T(8,128)S(1)} %get-tuple-element.42.dhs, f32[1048,512]{1,0:T(8,128)} %copy-done.16, f32[1024,512]{1,0:T(8,128)S(1)} %copy-done.6, ...), custom_call_target="tpu_custom_call" | custom-call | flops 471859200 | bytes 19394568 | tf_op jit(solution)/shard_map/leave/pallas_call | solution.py:294
  494.3 9.1 %add_reduce_fusion = (f32[1536]{0:T(1024)S(1)}, f32[1152,1536]{1,0:T(8,128)S(1)}) fusion(f32[1152,1536]{1,0:T(8,128)} %fusion.117, bf16[576,1536]{1,0:T(8,128)(2,1)} %copy-done.46, bf16[576,1536]{1,0:T(8,128)(2,1)S(1)} %copy-done.44, bf16[576,1536]{1,0:T(8,128)(2,1)} %get-tuple-element.114, bf16[576,1536]{1,0:T(8,128)(2,1)} %get-tuple-element.111, ...), kind=kOutput, calls=%fused_computation | convolution fusion | flops 3657693696 | bytes 26744832 | tf_op jit(solution)/shard_map/dot_general | solution.py:427
  516.0 3.4 fusion.10
  519.3 3.1 fusion.11
  523.0 3.0 pad_maximum_fusion
  526.0 8.1 %copy.76 = bf16[1728,1536]{0,1:T(8,128)(2,1)} copy(bf16[1728,1536]{1,0:T(8,128)(2,1)} %pad_maximum_fusion) | data formatting | bytes 10616832
  535.7 3.9 convolution_convert_fusion.3
  547.2 16.3 %collective-permute-done.18 = bf16[256,1536]{1,0:T(8,128)(2,1)S(1)} collective-permute-done((bf16[256,1536]{1,0:T(8,128)(2,1)}, bf16[256,1536]{1,0:T(8,128)(2,1)S(1)}, u32[]{:S(2)}, u32[]{:S(2)}) %collective-permute-start.18) | collective-permute-done | bytes 786464 | tf_op jit(solution)/shard_map/ppermute | solution.py:447
  565.8 15.5 %collective-permute-done.16 = bf16[256,1536]{1,0:T(8,128)(2,1)} collective-permute-done((bf16[256,1536]{1,0:T(8,128)(2,1)}, bf16[256,1536]{1,0:T(8,128)(2,1)}, u32[]{:S(2)}, u32[]{:S(2)}) %collective-permute-start.16) | collective-permute-done | bytes 786464 | tf_op jit(solution)/shard_map/ppermute | solution.py:447
  581.3 4.6 fusion.38
  593.6 3.5 fusion.37
  602.1 3.2 collective-permute-start.44
  605.3 3.4 fusion.35
  612.7 9.0 %collective-permute-done.43 = f32[144,128]{1,0:T(8,128)S(1)} collective-permute-done((f32[144,128]{1,0:T(8,128)S(1)}, f32[144,128]{1,0:T(8,128)S(1)}, u32[]{:S(2)}, u32[]{:S(2)}) %collective-permute-start.43) | collective-permute-done | bytes 73760 | tf_op jit(solution)/shard_map/ppermute | solution.py:438
  625.7 11.1 %collective-permute-done.30 = bf16[256,1536]{1,0:T(8,128)(2,1)} collective-permute-done((bf16[256,1536]{1,0:T(8,128)(2,1)}, bf16[256,1536]{1,0:T(8,128)(2,1)}, u32[]{:S(2)}, u32[]{:S(2)}) %collective-permute-start.30) | collective-permute-done | bytes 786464 | tf_op jit(solution)/shard_map/ppermute | solution.py:447
  636.9 2.8 fusion.46
  652.6 5.7 reduce-scatter.14.cloned.1.call-done
  658.3 2.7 copy.77
  (467 shorter events, 165.7 us)
Async XLA Ops:
  7.2 51.4 %all-gather.3.cloned.1.call-start = ((), (), s32[]{:S(2)}) async-start(), calls=%async_computation.3 | async-start | bytes 2150400 | tf_op jit(solution)/shard_map/all_gather | solution.py:645
  16.1 155.1 %all-gather.5.cloned.1.call-start = ((), (), s32[]{:S(2)}) async-start(), calls=%async_computation.4 | async-start | bytes 7618560 | tf_op jit(solution)/shard_map/all_gather | solution.py:648
  18.8 628.8 %reduce-scatter.12.cloned.1.call-start = ((), (), s32[]{:S(2)}) async-start(), calls=%async_computation.6 | async-start | bytes 983040
  19.6 153.3 %collective-permute-start = (bf16[128,1536]{1,0:T(8,128)(2,1)}, bf16[128,1536]{1,0:T(8,128)(2,1)}, u32[]{:S(2)}, u32[]{:S(2)}) collective-permute-start(bf16[128,1536]{1,0:T(8,128)(2,1)} %get-tuple-element.128), channel_id=1, source_target_pairs={{0,1},{1,0},{2,3},{3,2},{4,5},{5,4},{6,7},{7,6},{8,9},{9,8},{10,11... | collective-permute-start | bytes 1179656 | tf_op jit(solution)/shard_map/ppermute | solution.py:447
  58.6 118.8 %collective-permute-start.1 = (bf16[560,1536]{1,0:T(8,128)(2,1)}, bf16[560,1536]{1,0:T(8,128)(2,1)}, u32[]{:S(2)}, u32[]{:S(2)}) collective-permute-start(bf16[560,1536]{1,0:T(8,128)(2,1)} %all-gather.3.cloned.1.call-done), channel_id=1, source_target_pairs={{0,1},{1,0},{2,3},{3,2},{4,5},{5,4},{6,7},{7,6},{8,9},{9,8},{10,11... | collective-permute-start | bytes 5160968 | tf_op jit(solution)/shard_map/ppermute | solution.py:447
  171.2 96.2 %collective-permute-start.9 = (bf16[1984,1536]{1,0:T(8,128)(2,1)}, bf16[1984,1536]{1,0:T(8,128)(2,1)}, u32[]{:S(2)}, u32[]{:S(2)}) collective-permute-start(bf16[1984,1536]{1,0:T(8,128)(2,1)} %all-gather.5.cloned.1.call-done), channel_id=1, source_target_pairs={{0,1},{1,0},{2,3},{3,2},{4,5},{5,4},{6,7},{7,6},{8,9},{9,8},{10,11... | collective-permute-start | bytes 18284552 | tf_op jit(solution)/shard_map/ppermute | solution.py:447
  180.4 21.3 %collective-permute-start.4 = (bf16[256,1536]{1,0:T(8,128)(2,1)S(1)}, bf16[256,1536]{1,0:T(8,128)(2,1)S(1)}, u32[]{:S(2)}, u32[]{:S(2)}) collective-permute-start(bf16[256,1536]{1,0:T(8,128)(2,1)S(1)} %fusion.45), channel_id=1, source_target_pairs={{0,6},{1,7},{2,4},{3,5},{4,2},{5,3},{6,0},{7,1},{8,14},{9,15},{10,... | collective-permute-start | bytes 2359304 | tf_op jit(solution)/shard_map/ppermute | solution.py:447
  182.8 35.3 %collective-permute-start.3 = (bf16[256,1536]{1,0:T(8,128)(2,1)S(1)}, bf16[256,1536]{1,0:T(8,128)(2,1)S(1)}, u32[]{:S(2)}, u32[]{:S(2)}) collective-permute-start(bf16[256,1536]{1,0:T(8,128)(2,1)S(1)} %fusion.45), channel_id=1, source_target_pairs={{0,4},{1,5},{2,6},{3,7},{4,0},{5,1},{6,2},{7,3},{8,12},{9,13},{10,... | collective-permute-start | bytes 2359304 | tf_op jit(solution)/shard_map/ppermute | solution.py:447
  183.3 34.9 %collective-permute-start.2 = (bf16[256,1536]{1,0:T(8,128)(2,1)S(1)}, bf16[256,1536]{1,0:T(8,128)(2,1)}, u32[]{:S(2)}, u32[]{:S(2)}) collective-permute-start(bf16[256,1536]{1,0:T(8,128)(2,1)S(1)} %fusion.45), channel_id=1, source_target_pairs={{0,2},{1,3},{2,0},{3,1},{4,6},{5,7},{6,4},{7,5},{8,10},{9,11},{10,... | collective-permute-start | bytes 2359304 | tf_op jit(solution)/shard_map/ppermute | solution.py:447
  219.5 6.8 %collective-permute-start.5 = (bf16[8,1536]{1,0:T(8,128)(2,1)S(1)}, bf16[8,1536]{1,0:T(8,128)(2,1)S(1)}, u32[]{:S(2)}, u32[]{:S(2)}) collective-permute-start(bf16[8,1536]{1,0:T(8,128)(2,1)S(1)} %constant_dynamic-slice_fusion.2), channel_id=1, source_target_pairs={{0,8},{8,16},{16,24},{24,0},{1,9},{9,17},{17,25},{25,1},{2,10},{10... | collective-permute-start | bytes 73736 | tf_op jit(solution)/shard_map/ppermute | solution.py:438
  246.5 7.1 %collective-permute-start.6 = (f32[8,512]{1,0:T(8,128)S(1)}, f32[8,512]{1,0:T(8,128)S(1)}, u32[]{:S(2)}, u32[]{:S(2)}) collective-permute-start(f32[8,512]{1,0:T(8,128)S(1)} %get-tuple-element.39), channel_id=1, source_target_pairs={{0,8},{8,16},{16,24},{24,0},{1,9},{9,17},{17,25},{25,1},{2,10},{10... | collective-permute-start | bytes 49160 | tf_op jit(solution)/shard_map/ppermute | solution.py:438
  247.7 5.9 collective-permute-start.7
  270.6 19.6 %collective-permute-start.12 = (bf16[256,1536]{1,0:T(8,128)(2,1)S(1)}, bf16[256,1536]{1,0:T(8,128)(2,1)S(1)}, u32[]{:S(2)}, u32[]{:S(2)}) collective-permute-start(bf16[256,1536]{1,0:T(8,128)(2,1)S(1)} %convolution_convert_fusion), channel_id=1, source_target_pairs={{0,4},{1,5},{2,6},{3,7},{4,0},{5,1},{6,2},{7,3},{8,12},{9,13},{10,... | collective-permute-start | bytes 2359304 | tf_op jit(solution)/shard_map/ppermute | solution.py:447
  272.0 20.5 %collective-permute-start.11 = (bf16[256,1536]{1,0:T(8,128)(2,1)S(1)}, bf16[256,1536]{1,0:T(8,128)(2,1)S(1)}, u32[]{:S(2)}, u32[]{:S(2)}) collective-permute-start(bf16[256,1536]{1,0:T(8,128)(2,1)S(1)} %convolution_convert_fusion.1), channel_id=1, source_target_pairs={{0,2},{1,3},{2,0},{3,1},{4,6},{5,7},{6,4},{7,5},{8,10},{9,11},{10,... | collective-permute-start | bytes 2359304 | tf_op jit(solution)/shard_map/ppermute | solution.py:447
  272.8 33.3 %collective-permute-start.10 = (bf16[256,1536]{1,0:T(8,128)(2,1)S(1)}, bf16[256,1536]{1,0:T(8,128)(2,1)S(1)}, u32[]{:S(2)}, u32[]{:S(2)}) collective-permute-start(bf16[256,1536]{1,0:T(8,128)(2,1)S(1)} %convolution_convert_fusion.2), channel_id=1, source_target_pairs={{0,6},{1,7},{2,4},{3,5},{4,2},{5,3},{6,0},{7,1},{8,14},{9,15},{10,... | collective-permute-start | bytes 2359304 | tf_op jit(solution)/shard_map/ppermute | solution.py:447
  308.4 21.4 %collective-permute-start.15 = (bf16[256,1536]{1,0:T(8,128)(2,1)S(1)}, bf16[256,1536]{1,0:T(8,128)(2,1)S(1)}, u32[]{:S(2)}, u32[]{:S(2)}) collective-permute-start(bf16[256,1536]{1,0:T(8,128)(2,1)S(1)} %multiply_convert_fusion.2), channel_id=1, source_target_pairs={{0,6},{1,7},{2,4},{3,5},{4,2},{5,3},{6,0},{7,1},{8,14},{9,15},{10,... | collective-permute-start | bytes 2359304 | tf_op jit(solution)/shard_map/ppermute | solution.py:447
  309.9 32.5 %collective-permute-start.14 = (bf16[256,1536]{1,0:T(8,128)(2,1)S(1)}, bf16[256,1536]{1,0:T(8,128)(2,1)S(1)}, u32[]{:S(2)}, u32[]{:S(2)}) collective-permute-start(bf16[256,1536]{1,0:T(8,128)(2,1)S(1)} %multiply_convert_fusion.2), channel_id=1, source_target_pairs={{0,4},{1,5},{2,6},{3,7},{4,0},{5,1},{6,2},{7,3},{8,12},{9,13},{10,... | collective-permute-start | bytes 2359304 | tf_op jit(solution)/shard_map/ppermute | solution.py:447
  311.4 31.1 %collective-permute-start.13 = (bf16[256,1536]{1,0:T(8,128)(2,1)S(1)}, bf16[256,1536]{1,0:T(8,128)(2,1)S(1)}, u32[]{:S(2)}, u32[]{:S(2)}) collective-permute-start(bf16[256,1536]{1,0:T(8,128)(2,1)S(1)} %multiply_convert_fusion.2), channel_id=1, source_target_pairs={{0,2},{1,3},{2,0},{3,1},{4,6},{5,7},{6,4},{7,5},{8,10},{9,11},{10,... | collective-permute-start | bytes 2359304 | tf_op jit(solution)/shard_map/ppermute | solution.py:447
  370.3 19.5 %collective-permute-start.22 = (bf16[256,1536]{1,0:T(8,128)(2,1)S(1)}, bf16[256,1536]{1,0:T(8,128)(2,1)S(1)}, u32[]{:S(2)}, u32[]{:S(2)}) collective-permute-start(bf16[256,1536]{1,0:T(8,128)(2,1)S(1)} %fusion.41), channel_id=1, source_target_pairs={{0,4},{1,5},{2,6},{3,7},{4,0},{5,1},{6,2},{7,3},{8,12},{9,13},{10,... | collective-permute-start | bytes 2359304 | tf_op jit(solution)/shard_map/ppermute | solution.py:447
  373.0 20.5 %collective-permute-start.21 = (bf16[256,1536]{1,0:T(8,128)(2,1)S(1)}, bf16[256,1536]{1,0:T(8,128)(2,1)S(1)}, u32[]{:S(2)}, u32[]{:S(2)}) collective-permute-start(bf16[256,1536]{1,0:T(8,128)(2,1)S(1)} %fusion.40), channel_id=1, source_target_pairs={{0,2},{1,3},{2,0},{3,1},{4,6},{5,7},{6,4},{7,5},{8,10},{9,11},{10,... | collective-permute-start | bytes 2359304 | tf_op jit(solution)/shard_map/ppermute | solution.py:447
  374.9 34.2 %collective-permute-start.20 = (bf16[256,1536]{1,0:T(8,128)(2,1)S(1)}, bf16[256,1536]{1,0:T(8,128)(2,1)S(1)}, u32[]{:S(2)}, u32[]{:S(2)}) collective-permute-start(bf16[256,1536]{1,0:T(8,128)(2,1)S(1)} %fusion.39), channel_id=1, source_target_pairs={{0,6},{1,7},{2,4},{3,5},{4,2},{5,3},{6,0},{7,1},{8,14},{9,15},{10,... | collective-permute-start | bytes 2359304 | tf_op jit(solution)/shard_map/ppermute | solution.py:447
  411.2 21.4 %collective-permute-start.25 = (bf16[256,1536]{1,0:T(8,128)(2,1)S(1)}, bf16[256,1536]{1,0:T(8,128)(2,1)S(1)}, u32[]{:S(2)}, u32[]{:S(2)}) collective-permute-start(bf16[256,1536]{1,0:T(8,128)(2,1)S(1)} %fusion.112), channel_id=1, source_target_pairs={{0,6},{1,7},{2,4},{3,5},{4,2},{5,3},{6,0},{7,1},{8,14},{9,15},{10,... | collective-permute-start | bytes 2359304 | tf_op jit(solution)/shard_map/ppermute | solution.py:447
  412.6 34.8 %collective-permute-start.24 = (bf16[256,1536]{1,0:T(8,128)(2,1)S(1)}, bf16[256,1536]{1,0:T(8,128)(2,1)S(1)}, u32[]{:S(2)}, u32[]{:S(2)}) collective-permute-start(bf16[256,1536]{1,0:T(8,128)(2,1)S(1)} %fusion.112), channel_id=1, source_target_pairs={{0,4},{1,5},{2,6},{3,7},{4,0},{5,1},{6,2},{7,3},{8,12},{9,13},{10,... | collective-permute-start | bytes 2359304 | tf_op jit(solution)/shard_map/ppermute | solution.py:447
  414.2 33.1 %collective-permute-start.23 = (bf16[256,1536]{1,0:T(8,128)(2,1)S(1)}, bf16[256,1536]{1,0:T(8,128)(2,1)S(1)}, u32[]{:S(2)}, u32[]{:S(2)}) collective-permute-start(bf16[256,1536]{1,0:T(8,128)(2,1)S(1)} %fusion.112), channel_id=1, source_target_pairs={{0,2},{1,3},{2,0},{3,1},{4,6},{5,7},{6,4},{7,5},{8,10},{9,11},{10,... | collective-permute-start | bytes 2359304 | tf_op jit(solution)/shard_map/ppermute | solution.py:447
  422.1 93.9 %collective-permute-start.39 = (bf16[576,1536]{1,0:T(8,128)(2,1)}, bf16[576,1536]{1,0:T(8,128)(2,1)}, u32[]{:S(2)}, u32[]{:S(2)}) collective-permute-start(bf16[576,1536]{1,0:T(8,128)(2,1)} %slice.657), channel_id=1, source_target_pairs={{0,1},{1,0},{2,3},{3,2},{4,5},{5,4},{6,7},{7,6},{8,9},{9,8},{10,11... | collective-permute-start | bytes 5308424 | tf_op jit(solution)/shard_map/ppermute | solution.py:447
  456.5 12.9 %collective-permute-start.26 = (f32[8,512]{1,0:T(8,128)S(1)}, f32[8,512]{1,0:T(8,128)S(1)}, u32[]{:S(2)}, u32[]{:S(2)}) collective-permute-start(f32[8,512]{1,0:T(8,128)S(1)} %get-tuple-element.46), channel_id=1, source_target_pairs={{0,8},{8,16},{16,24},{24,0},{1,9},{9,17},{17,25},{25,1},{2,10},{10... | collective-permute-start | bytes 49160 | tf_op jit(solution)/shard_map/ppermute | solution.py:438
  459.1 10.2 %collective-permute-start.27 = (f32[8,512]{1,0:T(8,128)S(1)}, f32[8,512]{1,0:T(8,128)S(1)}, u32[]{:S(2)}, u32[]{:S(2)}) collective-permute-start(f32[8,512]{1,0:T(8,128)S(1)} %get-tuple-element.46), channel_id=1, source_target_pairs={{0,16},{8,24},{16,0},{24,8},{1,17},{9,25},{17,1},{25,9},{2,18},{10... | collective-permute-start | bytes 49160 | tf_op jit(solution)/shard_map/ppermute | solution.py:438
  459.5 9.9 %collective-permute-start.28 = (f32[8,512]{1,0:T(8,128)S(1)}, f32[8,512]{1,0:T(8,128)S(1)}, u32[]{:S(2)}, u32[]{:S(2)}) collective-permute-start(f32[8,512]{1,0:T(8,128)S(1)} %get-tuple-element.46), channel_id=1, source_target_pairs={{0,24},{8,0},{16,8},{24,16},{1,25},{9,1},{17,9},{25,17},{2,26},{10... | collective-permute-start | bytes 49160 | tf_op jit(solution)/shard_map/ppermute | solution.py:438
  485.4 7.5 %collective-permute-start.36 = (bf16[256,1536]{1,0:T(8,128)(2,1)S(1)}, bf16[256,1536]{1,0:T(8,128)(2,1)S(1)}, u32[]{:S(2)}, u32[]{:S(2)}) collective-permute-start(bf16[256,1536]{1,0:T(8,128)(2,1)S(1)} %slice.660), channel_id=1, source_target_pairs={{0,1},{1,0},{2,3},{3,2},{4,5},{5,4},{6,7},{7,6},{8,9},{9,8},{10,11... | collective-permute-start | bytes 2359304 | tf_op jit(solution)/shard_map/ppermute | solution.py:447
  491.9 13.4 %collective-permute-start.35 = (bf16[256,1536]{1,0:T(8,128)(2,1)}, bf16[256,1536]{1,0:T(8,128)(2,1)}, u32[]{:S(2)}, u32[]{:S(2)}) collective-permute-start(bf16[256,1536]{1,0:T(8,128)(2,1)} %slice.661), channel_id=1, source_target_pairs={{0,1},{1,0},{2,3},{3,2},{4,5},{5,4},{6,7},{7,6},{8,9},{9,8},{10,11... | collective-permute-start | bytes 2359304 | tf_op jit(solution)/shard_map/ppermute | solution.py:447
  492.4 17.4 %collective-permute-start.34 = (bf16[256,1536]{1,0:T(8,128)(2,1)}, bf16[256,1536]{1,0:T(8,128)(2,1)}, u32[]{:S(2)}, u32[]{:S(2)}) collective-permute-start(bf16[256,1536]{1,0:T(8,128)(2,1)} %slice.662), channel_id=1, source_target_pairs={{0,1},{1,0},{2,3},{3,2},{4,5},{5,4},{6,7},{7,6},{8,9},{9,8},{10,11... | collective-permute-start | bytes 2359304 | tf_op jit(solution)/shard_map/ppermute | solution.py:447
  494.2 155.2 %reduce-scatter.10.cloned.1.call-start = ((), (), s32[]{:S(2)}) async-start(), calls=%async_computation.5 | async-start | bytes 1966080
  504.9 14.4 %collective-permute-start.38 = (bf16[576,1536]{1,0:T(8,128)(2,1)}, bf16[576,1536]{1,0:T(8,128)(2,1)}, u32[]{:S(2)}, u32[]{:S(2)}) collective-permute-start(bf16[576,1536]{1,0:T(8,128)(2,1)} %slice.658), channel_id=1, source_target_pairs={{0,1},{1,0},{2,3},{3,2},{4,5},{5,4},{6,7},{7,6},{8,9},{9,8},{10,11... | collective-permute-start | bytes 5308424 | tf_op jit(solution)/shard_map/ppermute | solution.py:447
  513.0 145.3 %reduce-scatter.14.cloned.1.call-start = ((), (), s32[]{:S(2)}) async-start(), calls=%async_computation.7 | async-start | bytes 6881280
  515.4 7.0 %collective-permute-start.37 = (bf16[576,1536]{1,0:T(8,128)(2,1)S(1)}, bf16[576,1536]{1,0:T(8,128)(2,1)S(1)}, u32[]{:S(2)}, u32[]{:S(2)}) collective-permute-start(bf16[576,1536]{1,0:T(8,128)(2,1)S(1)} %slice.659), channel_id=1, source_target_pairs={{0,1},{1,0},{2,3},{3,2},{4,5},{5,4},{6,7},{7,6},{8,9},{9,8},{10,11... | collective-permute-start | bytes 5308424 | tf_op jit(solution)/shard_map/ppermute | solution.py:447
  543.7 19.8 %collective-permute-start.18 = (bf16[256,1536]{1,0:T(8,128)(2,1)}, bf16[256,1536]{1,0:T(8,128)(2,1)S(1)}, u32[]{:S(2)}, u32[]{:S(2)}) collective-permute-start(bf16[256,1536]{1,0:T(8,128)(2,1)} %convolution_convert_fusion.3), channel_id=1, source_target_pairs={{0,4},{1,5},{2,6},{3,7},{4,0},{5,1},{6,2},{7,3},{8,12},{9,13},{10,... | collective-permute-start | bytes 2359304 | tf_op jit(solution)/shard_map/ppermute | solution.py:447
  545.0 20.8 %collective-permute-start.17 = (bf16[256,1536]{1,0:T(8,128)(2,1)}, bf16[256,1536]{1,0:T(8,128)(2,1)}, u32[]{:S(2)}, u32[]{:S(2)}) collective-permute-start(bf16[256,1536]{1,0:T(8,128)(2,1)} %convolution_convert_fusion.4), channel_id=1, source_target_pairs={{0,2},{1,3},{2,0},{3,1},{4,6},{5,7},{6,4},{7,5},{8,10},{9,11},{10,... | collective-permute-start | bytes 2359304 | tf_op jit(solution)/shard_map/ppermute | solution.py:447
  545.8 35.6 %collective-permute-start.16 = (bf16[256,1536]{1,0:T(8,128)(2,1)}, bf16[256,1536]{1,0:T(8,128)(2,1)}, u32[]{:S(2)}, u32[]{:S(2)}) collective-permute-start(bf16[256,1536]{1,0:T(8,128)(2,1)} %convolution_convert_fusion.5), channel_id=1, source_target_pairs={{0,6},{1,7},{2,4},{3,5},{4,2},{5,3},{6,0},{7,1},{8,14},{9,15},{10,... | collective-permute-start | bytes 2359304 | tf_op jit(solution)/shard_map/ppermute | solution.py:447
  586.8 23.2 %collective-permute-start.19 = (bf16[128,1536]{1,0:T(8,128)(2,1)}, bf16[128,1536]{1,0:T(8,128)(2,1)}, u32[]{:S(2)}, u32[]{:S(2)}) collective-permute-start(bf16[128,1536]{1,0:T(8,128)(2,1)} %get-tuple-element.126), channel_id=1, source_target_pairs={{0,1},{1,0},{2,3},{3,2},{4,5},{5,4},{6,7},{7,6},{8,9},{9,8},{10,11... | collective-permute-start | bytes 1179656 | tf_op jit(solution)/shard_map/ppermute | solution.py:447
  593.3 8.3 %collective-permute-start.40 = (f32[2,128,256]{2,1,0:T(8,128)}, f32[2,128,256]{2,1,0:T(8,128)S(1)}, u32[]{:S(2)}, u32[]{:S(2)}) collective-permute-start(f32[2,128,256]{2,1,0:T(8,128)} %slice.444), channel_id=1, source_target_pairs={{0,1},{1,0},{2,3},{3,2},{4,5},{5,4},{6,7},{7,6},{8,9},{9,8},{10,11... | collective-permute-start | bytes 786440 | tf_op jit(solution)/shard_map/ppermute | solution.py:447
  597.1 28.7 %collective-permute-start.32 = (bf16[256,1536]{1,0:T(8,128)(2,1)}, bf16[256,1536]{1,0:T(8,128)(2,1)}, u32[]{:S(2)}, u32[]{:S(2)}) collective-permute-start(bf16[256,1536]{1,0:T(8,128)(2,1)} %fusion.37), channel_id=1, source_target_pairs={{0,4},{1,5},{2,6},{3,7},{4,0},{5,1},{6,2},{7,3},{8,12},{9,13},{10,... | collective-permute-start | bytes 2359304 | tf_op jit(solution)/shard_map/ppermute | solution.py:447
  599.9 25.8 %collective-permute-start.31 = (bf16[256,1536]{1,0:T(8,128)(2,1)}, bf16[256,1536]{1,0:T(8,128)(2,1)}, u32[]{:S(2)}, u32[]{:S(2)}) collective-permute-start(bf16[256,1536]{1,0:T(8,128)(2,1)} %fusion.36), channel_id=1, source_target_pairs={{0,2},{1,3},{2,0},{3,1},{4,6},{5,7},{6,4},{7,5},{8,10},{9,11},{10,... | collective-permute-start | bytes 2359304 | tf_op jit(solution)/shard_map/ppermute | solution.py:447
  602.1 7.8 %collective-permute-start.44 = (f32[144,128]{1,0:T(8,128)S(1)}, f32[144,128]{1,0:T(8,128)S(1)}, u32[]{:S(2)}, u32[]{:S(2)}) collective-permute-start(f32[144,128]{1,0:T(8,128)S(1)} %get-tuple-element.130), channel_id=1, source_target_pairs={{0,24},{8,0},{16,8},{24,16},{1,25},{9,1},{17,9},{25,17},{2,26},{10... | collective-permute-start | bytes 221192 | tf_op jit(solution)/shard_map/ppermute | solution.py:438
  608.7 28.2 %collective-permute-start.30 = (bf16[256,1536]{1,0:T(8,128)(2,1)}, bf16[256,1536]{1,0:T(8,128)(2,1)}, u32[]{:S(2)}, u32[]{:S(2)}) collective-permute-start(bf16[256,1536]{1,0:T(8,128)(2,1)} %fusion.35), channel_id=1, source_target_pairs={{0,6},{1,7},{2,4},{3,5},{4,2},{5,3},{6,0},{7,1},{8,14},{9,15},{10,... | collective-permute-start | bytes 2359304 | tf_op jit(solution)/shard_map/ppermute | solution.py:447
  610.0 11.7 %collective-permute-start.43 = (f32[144,128]{1,0:T(8,128)S(1)}, f32[144,128]{1,0:T(8,128)S(1)}, u32[]{:S(2)}, u32[]{:S(2)}) collective-permute-start(f32[144,128]{1,0:T(8,128)S(1)} %get-tuple-element.131), channel_id=1, source_target_pairs={{0,16},{8,24},{16,0},{24,8},{1,17},{9,25},{17,1},{25,9},{2,18},{10... | collective-permute-start | bytes 221192 | tf_op jit(solution)/shard_map/ppermute | solution.py:438
  610.0 11.7 %collective-permute-start.42 = (f32[144,128]{1,0:T(8,128)S(1)}, f32[144,128]{1,0:T(8,128)S(1)}, u32[]{:S(2)}, u32[]{:S(2)}) collective-permute-start(f32[144,128]{1,0:T(8,128)S(1)} %get-tuple-element.129), channel_id=1, source_target_pairs={{0,8},{8,16},{16,24},{24,0},{1,9},{9,17},{17,25},{25,1},{2,10},{10... | collective-permute-start | bytes 221192 | tf_op jit(solution)/shard_map/ppermute | solution.py:438
  624.2 18.1 %collective-permute-start.46 = (f32[2,384]{1,0:T(2,128)S(1)}, f32[2,384]{1,0:T(2,128)S(1)}, u32[]{:S(2)}, u32[]{:S(2)}) collective-permute-start(f32[2,384]{1,0:T(2,128)S(1)} %add.390), channel_id=1, source_target_pairs={{0,2},{1,3},{2,0},{3,1},{4,6},{5,7},{6,4},{7,5},{8,10},{9,11},{10,... | collective-permute-start | bytes 9224 | tf_op jit(solution)/shard_map/ppermute | solution.py:447
  641.5 5.0 collective-permute-start.33
  (102 other events, 1810.5 us)
Sparse Core Ops, SparseCore 0:
  16.2 42.3 all-gather.2
  60.2 110.9 all-gather.4
  494.4 23.2 reduce-scatter.11
  519.8 34.5 reduce-scatter.9
  556.5 101.7 reduce-scatter.13
